TPU v7x, 256 devices: a whole 4x4x8 slice. The times are simulated.
256 devices in a mesh: tm: 32 (over y, z_lo, core), space: 8 (over x, z_hi).
Axes of the slice: x: 4, y: 4, z: 8 (z_hi: 2, z_lo: 4; z = z_hi * 4 + z_lo), core: 2. Of those that a mesh axis runs over, the one named last changes fastest.
Arguments:
- nodes: float32 [32, 3, 32, 128, 256], P('tm', None, 'space'), may hold values from -6 to 6
- coefficients: bfloat16 [7, 32, 128, 256], P(None, 'space'), may hold values from -0.3 to 1, as said below
Outputs:
- new_nodes: float32 [32, 3, 32, 128, 256], P('tm', None, 'space')
Inputs may be any that keep to these rules, and one draw needn't show every extreme that they name: `coefficients`: entries 0 to 2 lie in [0.25, 1]; entry 3 is at most 0.3 sqrt(K0 K1) in magnitude, entry 4 0.3 sqrt(K0 K2), entry 5 0.3 sqrt(K1 K2); the rate lies in [0.02, 0.5].
All inputs are finite; a program needn't handle non-finite values.
Results may differ from a plain program's by a relative error of at most 0.0003.
Values sent between devices are 32-bit elements; how exact they have to be, the bound alone decides.
A program may use at most 64 MiB of HBM per device.

v0:
```python
import jax
import jax.numpy as jnp
from jax import lax
from jax.sharding import PartitionSpec as P

step_length = 0.2
node_step = 0.1
weight_a0 = 0.2 * 5.0 / 24.0
weight_a1 = 0.2 / 3.0
weight_a2 = -0.2 / 24.0
weight_b0 = -0.2 / 24.0
weight_b1 = 0.2 / 3.0
weight_b2 = 0.2 * 5.0 / 24.0


def padded_2(block, sides, width):
    for axis, dim in sides:
        count = lax.axis_size(axis)
        forward = [(i, i + 1) for i in range(count - 1)]
        backward = [(target, source) for source, target in forward]
        low = lax.ppermute(
            lax.slice_in_dim(block, block.shape[dim] - width, None, axis=dim), axis, forward
        )
        high = lax.ppermute(lax.slice_in_dim(block, 0, width, axis=dim), axis, backward)
        block = jnp.concatenate([low, block, high], axis=dim)
    return block


def shifted(value, axis, steps):
    count = lax.axis_size(axis)
    leading, last = (max(0, -steps), min(count, count - steps))
    return lax.ppermute(value, axis, [(source, source + steps) for source in range(leading, last)])


def operate(padded, coeffs, spacing):
    full = jnp.pad(padded, ((0, 0), (0, 0), (1, 1), (1, 1)))
    centre = full[:, 1:-1, 1:-1, 1:-1]
    second_z = full[:, 2:, 1:-1, 1:-1] - 2.0 * centre + full[:, :-2, 1:-1, 1:-1]
    second_x = (full[:, 1:-1, 2:, 1:-1] - 2.0 * centre + full[:, 1:-1, :-2, 1:-1]) / (
        spacing * spacing
    )
    second_y = (full[:, 1:-1, 1:-1, 2:] - 2.0 * centre + full[:, 1:-1, 1:-1, :-2]) / (
        spacing * spacing
    )
    cross_zx = (
        full[:, 2:, 2:, 1:-1]
        - full[:, 2:, :-2, 1:-1]
        - full[:, :-2, 2:, 1:-1]
        + full[:, :-2, :-2, 1:-1]
    ) / (2.0 * spacing)
    cross_zy = (
        full[:, 2:, 1:-1, 2:]
        - full[:, 2:, 1:-1, :-2]
        - full[:, :-2, 1:-1, 2:]
        + full[:, :-2, 1:-1, :-2]
    ) / (2.0 * spacing)
    cross_xy = (
        full[:, 1:-1, 2:, 2:]
        - full[:, 1:-1, 2:, :-2]
        - full[:, 1:-1, :-2, 2:]
        + full[:, 1:-1, :-2, :-2]
    ) / (2.0 * spacing * spacing)
    total = coeffs[0] * second_z + coeffs[1] * second_x + coeffs[2] * second_y
    total = total + coeffs[3] * cross_zx + coeffs[4] * cross_zy + coeffs[5] * cross_xy
    return total - coeffs[6] * centre


def restrict(field):
    summed = (
        field[..., 0::2, 0::2]
        + field[..., 0::2, 1::2]
        + field[..., 1::2, 0::2]
        + field[..., 1::2, 1::2]
    )
    return summed * 0.25


def prolong(field):
    return jnp.repeat(jnp.repeat(field, 2, axis=-2), 2, axis=-1)


def sweep_force(field, coeffs):
    rimmed = padded_2(field[None], (("space", 1),), 1)
    return operate(rimmed, coeffs, 1.0)[0]


def body(nodes, coefficients):
    coeffs = coefficients.astype(jnp.float32)
    coarse = restrict(coeffs)
    values = nodes[0]
    padded = padded_2(values, (("space", 1),), 1)
    forces = operate(padded, coeffs, 1.0)
    first = values[0] + (weight_a0 * forces[0] + weight_a1 * forces[1] + weight_a2 * forces[2])
    first_force = sweep_force(first, coeffs)
    last = (
        first
        + node_step * (first_force - forces[1])
        + (weight_b0 * forces[0] + weight_b1 * forces[1] + weight_b2 * forces[2])
    )
    last_force = sweep_force(last, coeffs)
    simpson = step_length * (forces[0] / 6.0 + first_force * (2.0 / 3.0) + last_force / 6.0)
    start_coarse = restrict(values[0])
    start_force = operate(restrict(padded[0:1]), coarse, 2.0)[0]
    constant = restrict(simpson) - step_length * start_force
    end_coarse = restrict(last)
    leading = lax.axis_index("tm") == 0

    def advance(start):
        rimmed = padded_2(start[None], (("space", 1),), 1)
        return start + step_length * operate(rimmed, coarse, 2.0)[0] + constant

    first_end = advance(start_coarse)

    def link(turn, carry):
        start, end = carry
        incoming = shifted(end, "tm", 1)
        start = jnp.where(leading, start_coarse, incoming)
        return (start, advance(start))

    start, end = lax.fori_loop(0, lax.axis_size("tm") - 1, link, (start_coarse, first_end))
    middle = first + prolong((start - start_coarse + (end - end_coarse)) * 0.5)
    final = last + prolong(end - end_coarse)
    received = shifted(final, "tm", 1)
    head = jnp.where(leading, values[0], received)
    return jnp.stack([head, middle, final])[None]


def solution(mesh):
    return jax.shard_map(
        body,
        mesh=mesh,
        in_specs=(P("tm", None, "space", None, None), P(None, "space", None, None)),
        out_specs=P("tm", None, "space", None, None),
        check_vma=False,
    )
```

profile of v0, /device:TPU:30, one launch (start us, length us, event | category | flops | bytes accessed | tf_op | source)
XLA Modules:
  0.0 1038.3 jit_solution(13323196323102077235)
XLA Ops:
  2.8 9.4 collective-permute-start.3
  33.8 8.7 collective-permute-start.7
  47.5 17.4 %slice.693 = f32[7,4,64,128]{2,3,1,0:T(8,128)} slice(bf16[7,4,128,256]{2,3,1,0:T(8,128)(2,1)S(1)} %copy.15), slice={[0:7:1], [0:4:1], [0:128:2], [0:256:2]} | slice | bytes 1835008 | tf_op jit(solution)/shard_map/slice | solution.py:70
  64.9 17.4 %slice.694 = f32[7,4,64,128]{2,3,1,0:T(8,128)} slice(bf16[7,4,128,256]{2,3,1,0:T(8,128)(2,1)S(1)} %copy.15), slice={[0:7:1], [0:4:1], [0:128:2], [1:256:2]} | slice | bytes 1835008 | tf_op jit(solution)/shard_map/slice | solution.py:71
  82.4 17.6 %slice.695 = f32[7,4,64,128]{2,3,1,0:T(8,128)} slice(bf16[7,4,128,256]{2,3,1,0:T(8,128)(2,1)S(1)} %copy.15), slice={[0:7:1], [0:4:1], [1:128:2], [0:256:2]} | slice | bytes 1835008 | tf_op jit(solution)/shard_map/slice | solution.py:72
  100.0 17.7 %slice.696 = f32[7,4,64,128]{2,3,1,0:T(8,128)} slice(bf16[7,4,128,256]{2,3,1,0:T(8,128)(2,1)S(1)} %copy.15), slice={[0:7:1], [0:4:1], [1:128:2], [1:256:2]} | slice | bytes 1835008 | tf_op jit(solution)/shard_map/slice | solution.py:73
  133.8 8.7 collective-permute-start.5
  151.4 8.2 slice.749
  159.6 8.2 slice.750
  167.8 8.3 slice.751
  176.1 8.3 slice.752
  194.7 9.1 collective-permute-start.9
  269.6 745.6 %while.14 = (s32[]{:T(128)}, f32[4,64,128]{2,1,0:T(8,128)}, f32[4,64,128]{2,1,0:T(8,128)}, pred[]{:T(512)}, f32[4,64,128]{2,1,0:T(8,128)}, /*index=5*/f32[7,4,64...) while((s32[]{:T(128)}, f32[4,64,128]{2,1,0:T(8,128)}, f32[4,64,128]{2,1,0:T(8,128)}, pred[]{:T(512)}, ...), condition=%wide.region_1.2_spmd, body=%wide.region_0.1_spmd.sunk | while | flops 2082922 | bytes 5842250 | solution.py:120
  278.9 7.8 collective-permute-start.1
  288.7 8.7 collective-permute-done.2
  300.6 7.3 collective-permute-done
  309.8 7.8 collective-permute-start.2
  323.7 7.6 collective-permute-done
  341.1 7.8 collective-permute-done.2
  352.1 7.6 collective-permute-done
  361.9 7.6 collective-permute-start.2
  375.9 7.6 collective-permute-done
  393.3 8.0 collective-permute-done.2
  404.5 7.6 collective-permute-done
  414.6 7.4 collective-permute-start.2
  428.5 7.6 collective-permute-done
  438.3 7.6 collective-permute-start.2
  452.3 7.6 collective-permute-done
  461.9 7.8 collective-permute-start.2
  475.7 7.6 collective-permute-done
  485.7 7.4 collective-permute-start.2
  499.6 7.6 collective-permute-done
  509.5 7.5 collective-permute-start.2
  523.5 7.6 collective-permute-done
  533.2 7.7 collective-permute-start.2
  547.1 7.6 collective-permute-done
  557.0 7.5 collective-permute-start.2
  570.9 7.6 collective-permute-done
  580.8 7.6 collective-permute-start.2
  594.7 7.6 collective-permute-done
  604.6 7.6 collective-permute-start.2
  618.4 7.6 collective-permute-done
  628.4 7.5 collective-permute-start.2
  642.2 7.6 collective-permute-done
  652.1 7.5 collective-permute-start.2
  666.0 7.6 collective-permute-done
  675.9 7.6 collective-permute-start.2
  689.7 7.6 collective-permute-done
  699.4 7.7 collective-permute-start.2
  737.5 7.4 collective-permute-done
  746.8 7.8 collective-permute-start.2
  760.8 7.4 collective-permute-done
  770.2 7.8 collective-permute-start.2
  793.6 7.8 collective-permute-start.2
  817.0 7.8 collective-permute-start.2
  840.1 7.8 collective-permute-start.2
  863.5 7.7 collective-permute-start.2
  886.6 7.8 collective-permute-start.2
  910.1 7.4 collective-permute-start.2
  933.3 7.7 collective-permute-start.2
  956.8 7.5 collective-permute-start.2
  980.1 7.7 collective-permute-start.2
  1003.3 7.7 collective-permute-start.2
  1025.4 9.9 collective-permute-done.11
  (421 shorter events, 504.2 us)
Async XLA Ops:
  2.8 122.3 %collective-permute-start.3 = (f32[3,1,128,256]{2,3,1,0:T(8,128)}, f32[3,1,128,256]{2,3,1,0:T(8,128)}, u32[]{:S(2)}, u32[]{:S(2)}) collective-permute-start(f32[3,1,128,256]{2,3,1,0:T(8,128)} %get-tuple-element.139), channel_id=1, source_target_pairs={{1,0},{2,1},{3,2},{4,3},{5,4},{6,5},{7,6},{9,8},{10,9},{11,10},{12... | collective-permute-start | bytes 1179656 | tf_op jit(solution)/shard_map/ppermute | solution.py:24
  12.2 112.9 %collective-permute-start.4 = (f32[3,1,128,256]{2,3,1,0:T(8,128)}, f32[3,1,128,256]{2,3,1,0:T(8,128)}, u32[]{:S(2)}, u32[]{:S(2)}) collective-permute-start(f32[3,1,128,256]{2,3,1,0:T(8,128)} %get-tuple-element.138), channel_id=1, source_target_pairs={{0,1},{1,2},{2,3},{3,4},{4,5},{5,6},{6,7},{8,9},{9,10},{10,11},{11... | collective-permute-start | bytes 1179656 | tf_op jit(solution)/shard_map/ppermute | solution.py:21
  33.8 114.3 %collective-permute-start.7 = (f32[1,1,64,128]{2,3,1,0:T(8,128)}, f32[1,1,64,128]{2,3,1,0:T(8,128)S(1)}, u32[]{:S(2)}, u32[]{:S(2)}) collective-permute-start(f32[1,1,64,128]{2,3,1,0:T(8,128)} %get-tuple-element.145), channel_id=1, source_target_pairs={{1,0},{2,1},{3,2},{4,3},{5,4},{6,5},{7,6},{9,8},{10,9},{11,10},{12... | collective-permute-start | bytes 98312 | tf_op jit(solution)/shard_map/ppermute | solution.py:24
  42.5 105.6 %collective-permute-start.8 = (f32[1,1,64,128]{2,3,1,0:T(8,128)}, f32[1,1,64,128]{2,3,1,0:T(8,128)}, u32[]{:S(2)}, u32[]{:S(2)}) collective-permute-start(f32[1,1,64,128]{2,3,1,0:T(8,128)} %get-tuple-element.144), channel_id=1, source_target_pairs={{0,1},{1,2},{2,3},{3,4},{4,5},{5,6},{6,7},{8,9},{9,10},{10,11},{11... | collective-permute-start | bytes 98312 | tf_op jit(solution)/shard_map/ppermute | solution.py:21
  133.8 50.7 %collective-permute-start.5 = (f32[1,1,128,256]{2,3,1,0:T(8,128)}, f32[1,1,128,256]{2,3,1,0:T(8,128)}, u32[]{:S(2)}, u32[]{:S(2)}) collective-permute-start(f32[1,1,128,256]{2,3,1,0:T(8,128)} %get-tuple-element.143), channel_id=1, source_target_pairs={{1,0},{2,1},{3,2},{4,3},{5,4},{6,5},{7,6},{9,8},{10,9},{11,10},{12... | collective-permute-start | bytes 393224 | tf_op jit(solution)/shard_map/ppermute | solution.py:24
  142.5 42.0 %collective-permute-start.6 = (f32[1,1,128,256]{2,3,1,0:T(8,128)}, f32[1,1,128,256]{2,3,1,0:T(8,128)}, u32[]{:S(2)}, u32[]{:S(2)}) collective-permute-start(f32[1,1,128,256]{2,3,1,0:T(8,128)} %get-tuple-element.142), channel_id=1, source_target_pairs={{0,1},{1,2},{2,3},{3,4},{4,5},{5,6},{6,7},{8,9},{9,10},{10,11},{11... | collective-permute-start | bytes 393224 | tf_op jit(solution)/shard_map/ppermute | solution.py:21
  192.8 36.1 %collective-permute-start.10 = (f32[1,1,128,256]{2,3,1,0:T(8,128)}, f32[1,1,128,256]{2,3,1,0:T(8,128)}, u32[]{:S(2)}, u32[]{:S(2)}) collective-permute-start(f32[1,1,128,256]{2,3,1,0:T(8,128)} %get-tuple-element.140), channel_id=1, source_target_pairs={{0,1},{1,2},{2,3},{3,4},{4,5},{5,6},{6,7},{8,9},{9,10},{10,11},{11... | collective-permute-start | bytes 393224 | tf_op jit(solution)/shard_map/ppermute | solution.py:21
  194.7 34.2 %collective-permute-start.9 = (f32[1,1,128,256]{2,3,1,0:T(8,128)}, f32[1,1,128,256]{2,3,1,0:T(8,128)}, u32[]{:S(2)}, u32[]{:S(2)}) collective-permute-start(f32[1,1,128,256]{2,3,1,0:T(8,128)} %get-tuple-element.141), channel_id=1, source_target_pairs={{1,0},{2,1},{3,2},{4,3},{5,4},{6,5},{7,6},{9,8},{10,9},{11,10},{12... | collective-permute-start | bytes 393224 | tf_op jit(solution)/shard_map/ppermute | solution.py:24
  278.9 9.8 collective-permute-start.1
  286.7 10.6 %collective-permute-start.2 = (f32[1,1,64,128]{3,2,1,0:T(8,128)S(1)}, f32[1,1,64,128]{3,2,1,0:T(8,128)S(1)}, u32[]{:S(2)}, u32[]{:S(2)}) collective-permute-start(f32[1,1,64,128]{3,2,1,0:T(8,128)S(1)} %get-tuple-element.190), channel_id=1, source_target_pairs={{0,1},{1,2},{2,3},{3,4},{4,5},{5,6},{6,7},{8,9},{9,10},{10,11},{11... | collective-permute-start | bytes 98312 | tf_op jit(solution)/shard_map/while/body/eval_jaxpr/ppermute | solution.py:21
  307.9 9.8 collective-permute-start.1
  309.8 10.6 %collective-permute-start.2 = (f32[1,1,64,128]{3,2,1,0:T(8,128)S(1)}, f32[1,1,64,128]{3,2,1,0:T(8,128)S(1)}, u32[]{:S(2)}, u32[]{:S(2)}) collective-permute-start(f32[1,1,64,128]{3,2,1,0:T(8,128)S(1)} %get-tuple-element.190), channel_id=1, source_target_pairs={{0,1},{1,2},{2,3},{3,4},{4,5},{5,6},{6,7},{8,9},{9,10},{10,11},{11... | collective-permute-start | bytes 98312 | tf_op jit(solution)/shard_map/while/body/eval_jaxpr/ppermute | solution.py:21
  331.3 9.8 collective-permute-start.1
  338.3 10.6 %collective-permute-start.2 = (f32[1,1,64,128]{3,2,1,0:T(8,128)S(1)}, f32[1,1,64,128]{3,2,1,0:T(8,128)S(1)}, u32[]{:S(2)}, u32[]{:S(2)}) collective-permute-start(f32[1,1,64,128]{3,2,1,0:T(8,128)S(1)} %get-tuple-element.190), channel_id=1, source_target_pairs={{0,1},{1,2},{2,3},{3,4},{4,5},{5,6},{6,7},{8,9},{9,10},{10,11},{11... | collective-permute-start | bytes 98312 | tf_op jit(solution)/shard_map/while/body/eval_jaxpr/ppermute | solution.py:21
  359.8 9.8 collective-permute-start.1
  361.9 10.8 %collective-permute-start.2 = (f32[1,1,64,128]{3,2,1,0:T(8,128)S(1)}, f32[1,1,64,128]{3,2,1,0:T(8,128)S(1)}, u32[]{:S(2)}, u32[]{:S(2)}) collective-permute-start(f32[1,1,64,128]{3,2,1,0:T(8,128)S(1)} %get-tuple-element.190), channel_id=1, source_target_pairs={{0,1},{1,2},{2,3},{3,4},{4,5},{5,6},{6,7},{8,9},{9,10},{10,11},{11... | collective-permute-start | bytes 98312 | tf_op jit(solution)/shard_map/while/body/eval_jaxpr/ppermute | solution.py:21
  383.5 9.8 collective-permute-start.1
  390.7 10.6 %collective-permute-start.2 = (f32[1,1,64,128]{3,2,1,0:T(8,128)S(1)}, f32[1,1,64,128]{3,2,1,0:T(8,128)S(1)}, u32[]{:S(2)}, u32[]{:S(2)}) collective-permute-start(f32[1,1,64,128]{3,2,1,0:T(8,128)S(1)} %get-tuple-element.190), channel_id=1, source_target_pairs={{0,1},{1,2},{2,3},{3,4},{4,5},{5,6},{6,7},{8,9},{9,10},{10,11},{11... | collective-permute-start | bytes 98312 | tf_op jit(solution)/shard_map/while/body/eval_jaxpr/ppermute | solution.py:21
  412.2 9.8 collective-permute-start.1
  414.6 10.7 %collective-permute-start.2 = (f32[1,1,64,128]{3,2,1,0:T(8,128)S(1)}, f32[1,1,64,128]{3,2,1,0:T(8,128)S(1)}, u32[]{:S(2)}, u32[]{:S(2)}) collective-permute-start(f32[1,1,64,128]{3,2,1,0:T(8,128)S(1)} %get-tuple-element.190), channel_id=1, source_target_pairs={{0,1},{1,2},{2,3},{3,4},{4,5},{5,6},{6,7},{8,9},{9,10},{10,11},{11... | collective-permute-start | bytes 98312 | tf_op jit(solution)/shard_map/while/body/eval_jaxpr/ppermute | solution.py:21
  438.3 10.7 %collective-permute-start.2 = (f32[1,1,64,128]{3,2,1,0:T(8,128)S(1)}, f32[1,1,64,128]{3,2,1,0:T(8,128)S(1)}, u32[]{:S(2)}, u32[]{:S(2)}) collective-permute-start(f32[1,1,64,128]{3,2,1,0:T(8,128)S(1)} %get-tuple-element.190), channel_id=1, source_target_pairs={{0,1},{1,2},{2,3},{3,4},{4,5},{5,6},{6,7},{8,9},{9,10},{10,11},{11... | collective-permute-start | bytes 98312 | tf_op jit(solution)/shard_map/while/body/eval_jaxpr/ppermute | solution.py:21
  459.9 9.8 collective-permute-start.1
  461.9 10.6 %collective-permute-start.2 = (f32[1,1,64,128]{3,2,1,0:T(8,128)S(1)}, f32[1,1,64,128]{3,2,1,0:T(8,128)S(1)}, u32[]{:S(2)}, u32[]{:S(2)}) collective-permute-start(f32[1,1,64,128]{3,2,1,0:T(8,128)S(1)} %get-tuple-element.190), channel_id=1, source_target_pairs={{0,1},{1,2},{2,3},{3,4},{4,5},{5,6},{6,7},{8,9},{9,10},{10,11},{11... | collective-permute-start | bytes 98312 | tf_op jit(solution)/shard_map/while/body/eval_jaxpr/ppermute | solution.py:21
  483.4 9.8 collective-permute-start.1
  485.7 10.7 %collective-permute-start.2 = (f32[1,1,64,128]{3,2,1,0:T(8,128)S(1)}, f32[1,1,64,128]{3,2,1,0:T(8,128)S(1)}, u32[]{:S(2)}, u32[]{:S(2)}) collective-permute-start(f32[1,1,64,128]{3,2,1,0:T(8,128)S(1)} %get-tuple-element.190), channel_id=1, source_target_pairs={{0,1},{1,2},{2,3},{3,4},{4,5},{5,6},{6,7},{8,9},{9,10},{10,11},{11... | collective-permute-start | bytes 98312 | tf_op jit(solution)/shard_map/while/body/eval_jaxpr/ppermute | solution.py:21
  509.5 10.7 %collective-permute-start.2 = (f32[1,1,64,128]{3,2,1,0:T(8,128)S(1)}, f32[1,1,64,128]{3,2,1,0:T(8,128)S(1)}, u32[]{:S(2)}, u32[]{:S(2)}) collective-permute-start(f32[1,1,64,128]{3,2,1,0:T(8,128)S(1)} %get-tuple-element.190), channel_id=1, source_target_pairs={{0,1},{1,2},{2,3},{3,4},{4,5},{5,6},{6,7},{8,9},{9,10},{10,11},{11... | collective-permute-start | bytes 98312 | tf_op jit(solution)/shard_map/while/body/eval_jaxpr/ppermute | solution.py:21
  531.2 9.8 collective-permute-start.1
  533.2 10.6 %collective-permute-start.2 = (f32[1,1,64,128]{3,2,1,0:T(8,128)S(1)}, f32[1,1,64,128]{3,2,1,0:T(8,128)S(1)}, u32[]{:S(2)}, u32[]{:S(2)}) collective-permute-start(f32[1,1,64,128]{3,2,1,0:T(8,128)S(1)} %get-tuple-element.190), channel_id=1, source_target_pairs={{0,1},{1,2},{2,3},{3,4},{4,5},{5,6},{6,7},{8,9},{9,10},{10,11},{11... | collective-permute-start | bytes 98312 | tf_op jit(solution)/shard_map/while/body/eval_jaxpr/ppermute | solution.py:21
  554.8 9.8 collective-permute-start.1
  557.0 10.7 %collective-permute-start.2 = (f32[1,1,64,128]{3,2,1,0:T(8,128)S(1)}, f32[1,1,64,128]{3,2,1,0:T(8,128)S(1)}, u32[]{:S(2)}, u32[]{:S(2)}) collective-permute-start(f32[1,1,64,128]{3,2,1,0:T(8,128)S(1)} %get-tuple-element.190), channel_id=1, source_target_pairs={{0,1},{1,2},{2,3},{3,4},{4,5},{5,6},{6,7},{8,9},{9,10},{10,11},{11... | collective-permute-start | bytes 98312 | tf_op jit(solution)/shard_map/while/body/eval_jaxpr/ppermute | solution.py:21
  578.6 9.8 collective-permute-start.1
  580.8 10.7 %collective-permute-start.2 = (f32[1,1,64,128]{3,2,1,0:T(8,128)S(1)}, f32[1,1,64,128]{3,2,1,0:T(8,128)S(1)}, u32[]{:S(2)}, u32[]{:S(2)}) collective-permute-start(f32[1,1,64,128]{3,2,1,0:T(8,128)S(1)} %get-tuple-element.190), channel_id=1, source_target_pairs={{0,1},{1,2},{2,3},{3,4},{4,5},{5,6},{6,7},{8,9},{9,10},{10,11},{11... | collective-permute-start | bytes 98312 | tf_op jit(solution)/shard_map/while/body/eval_jaxpr/ppermute | solution.py:21
  602.4 9.8 collective-permute-start.1
  604.6 10.6 %collective-permute-start.2 = (f32[1,1,64,128]{3,2,1,0:T(8,128)S(1)}, f32[1,1,64,128]{3,2,1,0:T(8,128)S(1)}, u32[]{:S(2)}, u32[]{:S(2)}) collective-permute-start(f32[1,1,64,128]{3,2,1,0:T(8,128)S(1)} %get-tuple-element.190), channel_id=1, source_target_pairs={{0,1},{1,2},{2,3},{3,4},{4,5},{5,6},{6,7},{8,9},{9,10},{10,11},{11... | collective-permute-start | bytes 98312 | tf_op jit(solution)/shard_map/while/body/eval_jaxpr/ppermute | solution.py:21
  626.1 9.8 collective-permute-start.1
  628.4 10.6 %collective-permute-start.2 = (f32[1,1,64,128]{3,2,1,0:T(8,128)S(1)}, f32[1,1,64,128]{3,2,1,0:T(8,128)S(1)}, u32[]{:S(2)}, u32[]{:S(2)}) collective-permute-start(f32[1,1,64,128]{3,2,1,0:T(8,128)S(1)} %get-tuple-element.190), channel_id=1, source_target_pairs={{0,1},{1,2},{2,3},{3,4},{4,5},{5,6},{6,7},{8,9},{9,10},{10,11},{11... | collective-permute-start | bytes 98312 | tf_op jit(solution)/shard_map/while/body/eval_jaxpr/ppermute | solution.py:21
  649.9 9.8 collective-permute-start.1
  652.1 10.6 %collective-permute-start.2 = (f32[1,1,64,128]{3,2,1,0:T(8,128)S(1)}, f32[1,1,64,128]{3,2,1,0:T(8,128)S(1)}, u32[]{:S(2)}, u32[]{:S(2)}) collective-permute-start(f32[1,1,64,128]{3,2,1,0:T(8,128)S(1)} %get-tuple-element.190), channel_id=1, source_target_pairs={{0,1},{1,2},{2,3},{3,4},{4,5},{5,6},{6,7},{8,9},{9,10},{10,11},{11... | collective-permute-start | bytes 98312 | tf_op jit(solution)/shard_map/while/body/eval_jaxpr/ppermute | solution.py:21
  673.7 9.8 collective-permute-start.1
  675.9 10.6 %collective-permute-start.2 = (f32[1,1,64,128]{3,2,1,0:T(8,128)S(1)}, f32[1,1,64,128]{3,2,1,0:T(8,128)S(1)}, u32[]{:S(2)}, u32[]{:S(2)}) collective-permute-start(f32[1,1,64,128]{3,2,1,0:T(8,128)S(1)} %get-tuple-element.190), channel_id=1, source_target_pairs={{0,1},{1,2},{2,3},{3,4},{4,5},{5,6},{6,7},{8,9},{9,10},{10,11},{11... | collective-permute-start | bytes 98312 | tf_op jit(solution)/shard_map/while/body/eval_jaxpr/ppermute | solution.py:21
  697.4 9.8 collective-permute-start.1
  699.4 10.7 %collective-permute-start.2 = (f32[1,1,64,128]{3,2,1,0:T(8,128)S(1)}, f32[1,1,64,128]{3,2,1,0:T(8,128)S(1)}, u32[]{:S(2)}, u32[]{:S(2)}) collective-permute-start(f32[1,1,64,128]{3,2,1,0:T(8,128)S(1)} %get-tuple-element.190), channel_id=1, source_target_pairs={{0,1},{1,2},{2,3},{3,4},{4,5},{5,6},{6,7},{8,9},{9,10},{10,11},{11... | collective-permute-start | bytes 98312 | tf_op jit(solution)/shard_map/while/body/eval_jaxpr/ppermute | solution.py:21
  720.7 9.8 collective-permute-start.1
  723.3 11.0 %collective-permute-start.2 = (f32[1,1,64,128]{3,2,1,0:T(8,128)S(1)}, f32[1,1,64,128]{3,2,1,0:T(8,128)S(1)}, u32[]{:S(2)}, u32[]{:S(2)}) collective-permute-start(f32[1,1,64,128]{3,2,1,0:T(8,128)S(1)} %get-tuple-element.190), channel_id=1, source_target_pairs={{0,1},{1,2},{2,3},{3,4},{4,5},{5,6},{6,7},{8,9},{9,10},{10,11},{11... | collective-permute-start | bytes 98312 | tf_op jit(solution)/shard_map/while/body/eval_jaxpr/ppermute | solution.py:21
  744.9 9.9 collective-permute-start.1
  746.8 10.8 %collective-permute-start.2 = (f32[1,1,64,128]{3,2,1,0:T(8,128)S(1)}, f32[1,1,64,128]{3,2,1,0:T(8,128)S(1)}, u32[]{:S(2)}, u32[]{:S(2)}) collective-permute-start(f32[1,1,64,128]{3,2,1,0:T(8,128)S(1)} %get-tuple-element.190), channel_id=1, source_target_pairs={{0,1},{1,2},{2,3},{3,4},{4,5},{5,6},{6,7},{8,9},{9,10},{10,11},{11... | collective-permute-start | bytes 98312 | tf_op jit(solution)/shard_map/while/body/eval_jaxpr/ppermute | solution.py:21
  768.2 9.9 collective-permute-start.1
  770.2 11.0 %collective-permute-start.2 = (f32[1,1,64,128]{3,2,1,0:T(8,128)S(1)}, f32[1,1,64,128]{3,2,1,0:T(8,128)S(1)}, u32[]{:S(2)}, u32[]{:S(2)}) collective-permute-start(f32[1,1,64,128]{3,2,1,0:T(8,128)S(1)} %get-tuple-element.190), channel_id=1, source_target_pairs={{0,1},{1,2},{2,3},{3,4},{4,5},{5,6},{6,7},{8,9},{9,10},{10,11},{11... | collective-permute-start | bytes 98312 | tf_op jit(solution)/shard_map/while/body/eval_jaxpr/ppermute | solution.py:21
  791.7 9.9 collective-permute-start.1
  793.6 10.9 %collective-permute-start.2 = (f32[1,1,64,128]{3,2,1,0:T(8,128)S(1)}, f32[1,1,64,128]{3,2,1,0:T(8,128)S(1)}, u32[]{:S(2)}, u32[]{:S(2)}) collective-permute-start(f32[1,1,64,128]{3,2,1,0:T(8,128)S(1)} %get-tuple-element.190), channel_id=1, source_target_pairs={{0,1},{1,2},{2,3},{3,4},{4,5},{5,6},{6,7},{8,9},{9,10},{10,11},{11... | collective-permute-start | bytes 98312 | tf_op jit(solution)/shard_map/while/body/eval_jaxpr/ppermute | solution.py:21
  815.0 9.9 collective-permute-start.1
  817.0 10.6 %collective-permute-start.2 = (f32[1,1,64,128]{3,2,1,0:T(8,128)S(1)}, f32[1,1,64,128]{3,2,1,0:T(8,128)S(1)}, u32[]{:S(2)}, u32[]{:S(2)}) collective-permute-start(f32[1,1,64,128]{3,2,1,0:T(8,128)S(1)} %get-tuple-element.190), channel_id=1, source_target_pairs={{0,1},{1,2},{2,3},{3,4},{4,5},{5,6},{6,7},{8,9},{9,10},{10,11},{11... | collective-permute-start | bytes 98312 | tf_op jit(solution)/shard_map/while/body/eval_jaxpr/ppermute | solution.py:21
  838.1 10.1 collective-permute-start.1
  840.1 10.8 %collective-permute-start.2 = (f32[1,1,64,128]{3,2,1,0:T(8,128)S(1)}, f32[1,1,64,128]{3,2,1,0:T(8,128)S(1)}, u32[]{:S(2)}, u32[]{:S(2)}) collective-permute-start(f32[1,1,64,128]{3,2,1,0:T(8,128)S(1)} %get-tuple-element.190), channel_id=1, source_target_pairs={{0,1},{1,2},{2,3},{3,4},{4,5},{5,6},{6,7},{8,9},{9,10},{10,11},{11... | collective-permute-start | bytes 98312 | tf_op jit(solution)/shard_map/while/body/eval_jaxpr/ppermute | solution.py:21
  861.4 9.8 collective-permute-start.1
  863.5 10.7 %collective-permute-start.2 = (f32[1,1,64,128]{3,2,1,0:T(8,128)S(1)}, f32[1,1,64,128]{3,2,1,0:T(8,128)S(1)}, u32[]{:S(2)}, u32[]{:S(2)}) collective-permute-start(f32[1,1,64,128]{3,2,1,0:T(8,128)S(1)} %get-tuple-element.190), channel_id=1, source_target_pairs={{0,1},{1,2},{2,3},{3,4},{4,5},{5,6},{6,7},{8,9},{9,10},{10,11},{11... | collective-permute-start | bytes 98312 | tf_op jit(solution)/shard_map/while/body/eval_jaxpr/ppermute | solution.py:21
  886.6 10.6 %collective-permute-start.2 = (f32[1,1,64,128]{3,2,1,0:T(8,128)S(1)}, f32[1,1,64,128]{3,2,1,0:T(8,128)S(1)}, u32[]{:S(2)}, u32[]{:S(2)}) collective-permute-start(f32[1,1,64,128]{3,2,1,0:T(8,128)S(1)} %get-tuple-element.190), channel_id=1, source_target_pairs={{0,1},{1,2},{2,3},{3,4},{4,5},{5,6},{6,7},{8,9},{9,10},{10,11},{11... | collective-permute-start | bytes 98312 | tf_op jit(solution)/shard_map/while/body/eval_jaxpr/ppermute | solution.py:21
  910.1 10.6 %collective-permute-start.2 = (f32[1,1,64,128]{3,2,1,0:T(8,128)S(1)}, f32[1,1,64,128]{3,2,1,0:T(8,128)S(1)}, u32[]{:S(2)}, u32[]{:S(2)}) collective-permute-start(f32[1,1,64,128]{3,2,1,0:T(8,128)S(1)} %get-tuple-element.190), channel_id=1, source_target_pairs={{0,1},{1,2},{2,3},{3,4},{4,5},{5,6},{6,7},{8,9},{9,10},{10,11},{11... | collective-permute-start | bytes 98312 | tf_op jit(solution)/shard_map/while/body/eval_jaxpr/ppermute | solution.py:21
  931.3 9.8 collective-permute-start.1
  933.3 10.7 %collective-permute-start.2 = (f32[1,1,64,128]{3,2,1,0:T(8,128)S(1)}, f32[1,1,64,128]{3,2,1,0:T(8,128)S(1)}, u32[]{:S(2)}, u32[]{:S(2)}) collective-permute-start(f32[1,1,64,128]{3,2,1,0:T(8,128)S(1)} %get-tuple-element.190), channel_id=1, source_target_pairs={{0,1},{1,2},{2,3},{3,4},{4,5},{5,6},{6,7},{8,9},{9,10},{10,11},{11... | collective-permute-start | bytes 98312 | tf_op jit(solution)/shard_map/while/body/eval_jaxpr/ppermute | solution.py:21
  956.8 10.6 %collective-permute-start.2 = (f32[1,1,64,128]{3,2,1,0:T(8,128)S(1)}, f32[1,1,64,128]{3,2,1,0:T(8,128)S(1)}, u32[]{:S(2)}, u32[]{:S(2)}) collective-permute-start(f32[1,1,64,128]{3,2,1,0:T(8,128)S(1)} %get-tuple-element.190), channel_id=1, source_target_pairs={{0,1},{1,2},{2,3},{3,4},{4,5},{5,6},{6,7},{8,9},{9,10},{10,11},{11... | collective-permute-start | bytes 98312 | tf_op jit(solution)/shard_map/while/body/eval_jaxpr/ppermute | solution.py:21
  980.1 10.6 %collective-permute-start.2 = (f32[1,1,64,128]{3,2,1,0:T(8,128)S(1)}, f32[1,1,64,128]{3,2,1,0:T(8,128)S(1)}, u32[]{:S(2)}, u32[]{:S(2)}) collective-permute-start(f32[1,1,64,128]{3,2,1,0:T(8,128)S(1)} %get-tuple-element.190), channel_id=1, source_target_pairs={{0,1},{1,2},{2,3},{3,4},{4,5},{5,6},{6,7},{8,9},{9,10},{10,11},{11... | collective-permute-start | bytes 98312 | tf_op jit(solution)/shard_map/while/body/eval_jaxpr/ppermute | solution.py:21
  1003.3 10.6 %collective-permute-start.2 = (f32[1,1,64,128]{3,2,1,0:T(8,128)S(1)}, f32[1,1,64,128]{3,2,1,0:T(8,128)S(1)}, u32[]{:S(2)}, u32[]{:S(2)}) collective-permute-start(f32[1,1,64,128]{3,2,1,0:T(8,128)S(1)} %get-tuple-element.190), channel_id=1, source_target_pairs={{0,1},{1,2},{2,3},{3,4},{4,5},{5,6},{6,7},{8,9},{9,10},{10,11},{11... | collective-permute-start | bytes 98312 | tf_op jit(solution)/shard_map/while/body/eval_jaxpr/ppermute | solution.py:21
  1021.8 13.5 %collective-permute-start.11 = (f32[4,128,256]{1,2,0:T(8,128)}, f32[4,128,256]{1,2,0:T(8,128)}, u32[]{:S(2)}, u32[]{:S(2)}) collective-permute-start(f32[4,128,256]{1,2,0:T(8,128)} %add.484), channel_id=1, source_target_pairs={{0,8},{8,16},{16,24},{24,32},{32,40},{40,48},{48,56},{56,64},{64,7... | collective-permute-start | bytes 1572872 | tf_op jit(solution)/shard_map/ppermute | solution.py:32
  (83 other events, 906.1 us)
where the time goes:
time: 1050 us; the launch traced here: 1040 us
  starting transfers between devices  407 us (39%)
  waiting for transfers between devices  351 us (33%)
  local copies, waits for them, and re-layouts  195 us (19%)
  other arithmetic  81.8 us (8%)
    ppermute x32, waiting for transfers between devices, shifted(): lax.ppermute(value, axis, [(source, source + steps) for source in range(l...  241 us
    ppermute x35, starting transfers between devices, padded_2(): lax.ppermute(lax.slice_in_dim(block, block.shape[dim] - width, None, axis...  229 us
    ppermute x35, starting transfers between devices, padded_2(): lax.ppermute(lax.slice_in_dim(block, 0, width, axis=dim), axis, backward)  117 us
    ppermute x35, waiting for transfers between devices, padded_2(): lax.ppermute(lax.slice_in_dim(block, block.shape[dim] - width, None, axis...  109 us
    ppermute x32, starting transfers between devices, shifted(): lax.ppermute(value, axis, [(source, source + steps) for source in range(l...  61.1 us
    slice x5, local copies, waits for them, and re-layouts, restrict(): field[..., 1::2, 1::2]  42.7 us
    slice x5, local copies, waits for them, and re-layouts, restrict(): field[..., 1::2, 0::2]  42.6 us
    slice x5, local copies, waits for them, and re-layouts, restrict(): field[..., 0::2, 1::2]  42.4 us
  transfers between devices with their start and end apart: 102, of which 77 were waited for; matrix products, arithmetic and copies ran while one was open for 17% of the time, Pallas kernels for 0%

commit v1 on v0

v1 whole, which is shorter than its diff:
```python
import functools

import jax
import jax.numpy as jnp
from jax import lax
from jax.experimental import pallas as pl
from jax.experimental.pallas import tpu as pltpu
from jax.sharding import PartitionSpec as P

MESH = pl.DeviceIdType.MESH
F32 = jnp.float32
HIGH = lax.Precision.HIGHEST

A0, A1, A2 = 0.2 * 5.0 / 24.0, 0.2 / 3.0, -0.2 / 24.0
B0, B1, B2 = -0.2 / 24.0, 0.2 / 3.0, 0.2 * 5.0 / 24.0
C0, C1 = 0.2 / 6.0, 0.2 * 2.0 / 3.0

DEPTH = 4
ROWS, COLS = 128, 256
HALF, LANES = 64, 128
SLABS = 8
BLOCK = 8
NT = 32
RIM = 8
STRIP = 32
WIN = 24


def worker_place(j):
    return 6 - 6 * lax.rem(j, 2)


def neighbours(value, axis, size, mask_low, mask_high):
    ahead = pltpu.roll(value, size - 1, axis)
    behind = pltpu.roll(value, 1, axis)
    return jnp.where(mask_high, 0.0, ahead), jnp.where(mask_low, 0.0, behind)


def rows_around(value, size):
    return pltpu.roll(value, size - 1, 0), pltpu.roll(value, 1, 0)


def stencil(low, here, high, k, height, width, top, rows):
    lane = lax.broadcasted_iota(jnp.int32, (height, width), 1)
    first, last = lane == 0, lane == width - 1
    cut = lambda v: v[top : top + rows]
    over_z = high - low
    right, left = neighbours(here, 1, width, first, last)
    slope = right - left
    d_right, d_left = neighbours(over_z, 1, width, first, last)
    down, up = rows_around(here, height)
    z_down, z_up = rows_around(over_z, height)
    s_down, s_up = rows_around(slope, height)
    total = k[0] * cut(high + low) + k[1] * cut(down + up) + k[2] * cut(right + left)
    total = total + k[3] * cut(z_down - z_up) + k[4] * cut(d_right - d_left)
    total = total + k[5] * cut(s_down - s_up)
    return total + k[6] * cut(here)


def pair_matrix(shape, long_axis, value):
    long = lax.broadcasted_iota(jnp.int32, shape, long_axis)
    short = lax.broadcasted_iota(jnp.int32, shape, 1 - long_axis)
    return jnp.where((long == 2 * short) | (long == 2 * short + 1), value, 0.0).astype(F32)


def restrict(plane):
    across = jnp.dot(plane, pair_matrix((COLS, LANES), 0, 0.5), precision=HIGH, preferred_element_type=F32)
    return jnp.dot(pair_matrix((HALF, ROWS), 1, 0.5), across, precision=HIGH, preferred_element_type=F32)


def prolong(plane):
    along = jnp.dot(pair_matrix((ROWS, HALF), 0, 1.0), plane, precision=HIGH, preferred_element_type=F32)
    return jnp.dot(along, pair_matrix((LANES, COLS), 1, 1.0), precision=HIGH, preferred_element_type=F32)


def loop(count, fn, unroll=1):
    def step(i, carry):
        fn(i)
        return carry

    lax.fori_loop(0, count, step, 0, unroll=unroll)


def kernel(
    nodes, coeffs, out,
    kf, ab, bb, cb, v1, v2, v2p, kcp, rp, w0, wn, kb, rb, hb, ec, en,
    halo_s, halo_r, shift_s, shift_r, k_s, k_r, r_s, r_r, hand_s, hand_r, e_s, e_r, f_s, f_r, known,
):
    t = lax.axis_index("tm")
    s = lax.axis_index("space")
    block = lax.div(t, BLOCK)
    place = lax.rem(t, BLOCK)
    base = block * BLOCK
    is_worker = place == worker_place(s)
    strips = ROWS // STRIP

    def tell(sem, tm, sp):
        pl.semaphore_signal(sem, inc=1, device_id=(tm, sp), device_id_type=MESH)

    barrier = pltpu.get_barrier_semaphore()
    for n in range(1, SLABS):
        tell(barrier, t, lax.rem(s + n, SLABS))
    for n in range(1, BLOCK):
        tell(barrier, base + lax.rem(place + n, BLOCK), s)

    cross_up = (place == BLOCK - 1) & (t < NT - 1)
    cross_down = (place == 0) & (t > 0)

    @pl.when(cross_up)
    def _():
        tell(barrier, t + 1, s)

    @pl.when(cross_down)
    def _():
        tell(barrier, t - 1, s)

    for dj in (-1, 0, 1):
        j = s + dj

        @pl.when(is_worker & (block > 0) & (j >= 0) & (j < SLABS))
        def _(j=j):
            tell(barrier, base - BLOCK + worker_place(j), j)

    for buf in (ab, bb, cb):
        buf[:, 0:RIM, :] = jnp.zeros((DEPTH + 2, RIM, COLS), F32)
        buf[:, RIM + ROWS :, :] = jnp.zeros((DEPTH + 2, RIM, COLS), F32)

    @pl.when(s == 0)
    def _():
        for buf in (ab, bb, cb):
            buf[0, RIM : RIM + ROWS, :] = jnp.zeros((ROWS, COLS), F32)

    @pl.when(s == SLABS - 1)
    def _():
        for buf in (ab, bb, cb):
            buf[DEPTH + 1, RIM : RIM + ROWS, :] = jnp.zeros((ROWS, COLS), F32)

    kcp[:, :, 0:RIM, :] = jnp.zeros((7, DEPTH, RIM, LANES), F32)
    kcp[:, :, RIM + HALF :, :] = jnp.zeros((7, DEPTH, RIM, LANES), F32)
    rp[:, 0:RIM, :] = jnp.zeros((DEPTH, RIM, LANES), F32)
    rp[:, RIM + HALF :, :] = jnp.zeros((DEPTH, RIM, LANES), F32)

    def combine_a(p, i):
        here = pl.ds(pl.multiple_of(i * STRIP, STRIP), STRIP)
        there = pl.ds(pl.multiple_of(RIM + i * STRIP, 8), STRIP)
        ab[p + 1, there, :] = A0 * nodes[0, 0, p, here, :] + A1 * nodes[0, 1, p, here, :] + A2 * nodes[0, 2, p, here, :]

    loop(strips, lambda i: combine_a(0, i))
    loop(strips, lambda i: combine_a(3, i))

    expect = 14 + jnp.where(cross_up, 1, 0) + jnp.where(cross_down, 1, 0)
    hands = 3 - jnp.where(s == 0, 1, 0) - jnp.where(s == SLABS - 1, 1, 0)
    expect = expect + jnp.where(is_worker & (block < NT // BLOCK - 1), hands, 0)
    pl.semaphore_wait(barrier, expect)

    inner = pl.ds(RIM, ROWS)

    def halo(buf, phase, upward):
        return pltpu.make_async_remote_copy(
            src_ref=buf.at[DEPTH if upward else 1, inner],
            dst_ref=buf.at[0 if upward else DEPTH + 1, inner],
            send_sem=halo_s.at[phase, int(upward)],
            recv_sem=halo_r.at[phase, int(upward)],
            device_id=(t, s + 1 if upward else s - 1),
            device_id_type=MESH,
        )

    def send_halo(buf, phase, upward):
        @pl.when(s < SLABS - 1 if upward else s > 0)
        def _():
            halo(buf, phase, upward).start()

    def take_halo(buf, phase, upward):
        @pl.when(s > 0 if upward else s < SLABS - 1)
        def _():
            halo(buf, phase, upward).wait_recv()

    send_halo(ab, 0, False)
    send_halo(ab, 0, True)
    for n in range(1, BLOCK):
        tell(known, base + lax.rem(place + n, BLOCK), s)

    def shift(src, dst, n, tm):
        return pltpu.make_async_remote_copy(
            src_ref=src, dst_ref=dst, send_sem=shift_s.at[n], recv_sem=shift_r.at[n],
            device_id=(tm, s), device_id_type=MESH,
        )

    send_w0 = shift(w0, wn, 0, t - 1)
    send_v2 = shift(v2, v2p, 1, t + 1)

    def start_coarse(p):
        w0[p] = restrict(nodes[0, 0, p])

    loop(DEPTH, start_coarse)

    @pl.when(t > 0)
    def _():
        send_w0.start()

    @pl.when(t == NT - 1)
    def _():
        wn[...] = jnp.zeros_like(wn)

    def weights(p, i):
        here = pl.ds(pl.multiple_of(i * STRIP, STRIP), STRIP)
        k = [coeffs[m, p, here, :].astype(F32) for m in range(7)]
        for m in range(3):
            kf[m, p, here, :] = k[m]
            kf[3 + m, p, here, :] = 0.5 * k[3 + m]
        kf[6, p, here, :] = -(2.0 * (k[0] + k[1] + k[2]) + k[6])

    loop(DEPTH * strips, lambda n: weights(lax.div(n, strips), lax.rem(n, strips)))
    loop(strips, lambda i: combine_a(1, i))
    loop(strips, lambda i: combine_a(2, i))

    def force(buf, p, i):
        window = pl.ds(pl.multiple_of(i * STRIP, STRIP), STRIP + 2 * RIM)
        here = pl.ds(pl.multiple_of(i * STRIP, STRIP), STRIP)
        return stencil(
            buf[p, window, :], buf[p + 1, window, :], buf[p + 2, window, :],
            [kf[m, p, here, :] for m in range(7)], STRIP + 2 * RIM, COLS, RIM, STRIP,
        )

    def spots(i):
        return (
            pl.ds(pl.multiple_of(i * STRIP, STRIP), STRIP),
            pl.ds(pl.multiple_of(RIM + i * STRIP, 8), STRIP),
        )

    def first_node(p, i):
        here, there = spots(i)
        value = nodes[0, 0, p, here, :] + force(ab, p, i)
        v1[p, here, :] = value
        bb[p + 1, there, :] = (
            0.1 * value + B0 * nodes[0, 0, p, here, :] + (B1 - 0.1) * nodes[0, 1, p, here, :] + B2 * nodes[0, 2, p, here, :]
        )

    def last_node(p, i):
        here, there = spots(i)
        first = v1[p, here, :]
        value = first + force(bb, p, i)
        v2[p, here, :] = value
        cb[p + 1, there, :] = C0 * (nodes[0, 0, p, here, :] + value) + C1 * first

    def add_force(p, i):
        here, there = spots(i)
        out[0, 0, p, here, :] = nodes[0, 0, p, here, :] + force(cb, p, i)

    def planes(fn, which):
        for p in which:
            loop(strips, lambda i, p=p: fn(p, i))

    def coarse_weights(n):
        m, p = lax.div(n, DEPTH), lax.rem(n, DEPTH)
        plane = coeffs[m, p].astype(F32)
        kcp[m, p, RIM : RIM + HALF, :] = restrict(plane)

    loop(7 * DEPTH, coarse_weights)

    def scale_weights(p):
        here = slice(RIM, RIM + HALF)
        k = [kcp[m, p, here, :] for m in range(7)]
        kcp[0, p, here, :] = 0.2 * k[0]
        for m in range(1, 5):
            kcp[m, p, here, :] = 0.05 * k[m]
        kcp[5, p, here, :] = 0.025 * k[5]
        kcp[6, p, here, :] = 1.0 - (0.4 * k[0] + 0.1 * (k[1] + k[2]) + 0.2 * k[6])

    loop(DEPTH, scale_weights)
    planes(first_node, (1, 2))
    pl.semaphore_wait(known, BLOCK - 1)

    goal = worker_place(place)
    k_self = (goal == place) & (place == s)
    window = pl.ds(pl.multiple_of(8 * place, 8), WIN)
    slab = pl.ds(pl.multiple_of(DEPTH * s, DEPTH), DEPTH)
    send_k = pltpu.make_async_remote_copy(
        src_ref=kcp.at[:, :, window], dst_ref=kb.at[:, slab], send_sem=k_s.at[0], recv_sem=k_r.at[0],
        device_id=(base + goal, place), device_id_type=MESH,
    )

    @pl.when(k_self)
    def _():
        pltpu.make_async_copy(kcp.at[:, :, window], kb.at[:, slab], k_r.at[0]).start()

    @pl.when(jnp.logical_not(k_self))
    def _():
        send_k.start()

    take_halo(ab, 0, True)
    planes(first_node, (0,))
    send_halo(bb, 1, False)
    take_halo(ab, 0, False)
    planes(first_node, (3,))
    send_halo(bb, 1, True)
    planes(last_node, (1, 2))
    take_halo(bb, 1, True)
    planes(last_node, (0,))
    send_halo(cb, 2, False)
    take_halo(bb, 1, False)
    planes(last_node, (3,))
    send_halo(cb, 2, True)

    @pl.when(t < NT - 1)
    def _():
        send_v2.start()

    planes(add_force, (1, 2))
    take_halo(cb, 2, True)
    planes(add_force, (0,))
    take_halo(cb, 2, False)
    planes(add_force, (3,))

    @pl.when(t < NT - 1)
    def _():
        send_w0.wait_recv()

    def right_side(p):
        rp[p, RIM : RIM + HALF, :] = restrict(out[0, 0, p]) - wn[p]

    loop(DEPTH, right_side)

    def send_r(j):
        to = worker_place(j)
        rows = pl.ds(pl.multiple_of(8 * j, 8), WIN)
        own = (to == place) & (j == s)
        copy = pltpu.make_async_remote_copy(
            src_ref=rp.at[:, rows], dst_ref=rb.at[place, slab], send_sem=r_s.at[j], recv_sem=r_r.at[place],
            device_id=(base + to, j), device_id_type=MESH,
        )
        return own, copy, pltpu.make_async_copy(rp.at[:, rows], rb.at[place, slab], r_r.at[place])

    def start_r(j):
        own, copy, local = send_r(j)

        @pl.when(own)
        def _():
            local.start()

        @pl.when(jnp.logical_not(own))
        def _():
            copy.start()

    loop(SLABS, start_r)

    @pl.when(t > 0)
    def _():
        send_v2.wait_recv()

    def early(p):
        @pl.when(t > 0)
        def _():
            out[0, 0, p] = v2p[p] + prolong(restrict(nodes[0, 0, p] - v2p[p]))

        @pl.when(t == 0)
        def _():
            out[0, 0, p] = nodes[0, 0, p]

        gap = prolong(wn[p] - restrict(v2[p]))
        out[0, 1, p] = v1[p] + 0.5 * gap
        out[0, 2, p] = v2[p] + gap

    loop(DEPTH, early)

    def hand(dj):
        j = s + dj
        return pltpu.make_async_remote_copy(
            src_ref=hb.at[BLOCK, pl.ds(1, 32), pl.ds(8, 8)],
            dst_ref=hb.at[0, pl.ds(1, 32), pl.ds(8 - 8 * dj, 8)],
            send_sem=hand_s.at[dj + 1],
            recv_sem=hand_r.at[dj + 1],
            device_id=(base + BLOCK + worker_place(j), j),
            device_id_type=MESH,
        )

    def spread(h, to):
        src = hb.at[h + 1, pl.ds(1 + DEPTH * to, DEPTH), pl.ds(8, 8)]
        dst = en.at[:, pl.ds(pl.multiple_of(8 * s, 8), 8)]
        own = (h == place) & (to == s)
        copy = pltpu.make_async_remote_copy(
            src_ref=src, dst_ref=dst, send_sem=e_s.at[h, to], recv_sem=e_r.at[0],
            device_id=(base + h, to), device_id_type=MESH,
        )
        return own, copy, pltpu.make_async_copy(src, dst, e_r.at[0])

    def start_spread(h):
        def one(to):
            own, copy, local = spread(h, to)

            @pl.when(own)
            def _():
                local.start()

            @pl.when(jnp.logical_not(own))
            def _():
                copy.start()

        loop(SLABS, one)

    @pl.when(is_worker)
    def _():
        def clear(h):
            hb[h, 0] = jnp.zeros((WIN, LANES), F32)
            hb[h, 33] = jnp.zeros((WIN, LANES), F32)

        loop(BLOCK + 1, clear)

        @pl.when(block == 0)
        def _():
            hb[0, 1:33] = jnp.zeros((32, WIN, LANES), F32)

        @pl.when((block > 0) & (s == 0))
        def _():
            hb[0, 1:33, 0:8, :] = jnp.zeros((32, 8, LANES), F32)

        @pl.when((block > 0) & (s == SLABS - 1))
        def _():
            hb[0, 1:33, 16:24, :] = jnp.zeros((32, 8, LANES), F32)

        pltpu.make_async_copy(kb, kb, k_r.at[0]).wait()
        for dj in (-1, 0, 1):
            @pl.when((block > 0) & (s - dj >= 0) & (s - dj < SLABS))
            def _(dj=dj):
                hand(dj).wait_recv()

        def advance(h):
            pltpu.make_async_copy(rb.at[h], rb.at[h], r_r.at[h]).wait()

            def plane(p):
                value = stencil(
                    hb[h, p], hb[h, p + 1], hb[h, p + 2],
                    [kb[m, p] for m in range(7)], WIN, LANES, 0, WIN,
                )
                hb[h + 1, p + 1] = value + rb[h, p]

            loop(32, plane, unroll=2)

            @pl.when(block == NT // BLOCK - 1)
            def _():
                start_spread(h)

        loop(BLOCK, advance)

        @pl.when(block < NT // BLOCK - 1)
        def _():
            for dj in (-1, 0, 1):
                j = s + dj

                @pl.when((j >= 0) & (j < SLABS))
                def _(dj=dj):
                    hand(dj).start()

            loop(BLOCK, start_spread)

    pltpu.make_async_copy(en, en, e_r.at[0]).wait()
    forward = pltpu.make_async_remote_copy(
        src_ref=en, dst_ref=ec, send_sem=f_s.at[0], recv_sem=f_r.at[0], device_id=(t + 1, s), device_id_type=MESH
    )

    @pl.when(t < NT - 1)
    def _():
        forward.start()

    def end_node(p):
        gain = prolong(en[p])
        out[0, 2, p] += gain
        out[0, 1, p] += 0.5 * gain

    loop(DEPTH, end_node)

    @pl.when(t > 0)
    def _():
        forward.wait_recv()

        def start_node(p):
            gain = prolong(ec[p])
            out[0, 0, p] += gain
            out[0, 1, p] += 0.5 * gain

        loop(DEPTH, start_node)

    for phase, buf in enumerate((ab, bb, cb)):

        @pl.when(s < SLABS - 1)
        def _(phase=phase, buf=buf):
            halo(buf, phase, True).wait_send()

        @pl.when(s > 0)
        def _(phase=phase, buf=buf):
            halo(buf, phase, False).wait_send()

    @pl.when(t > 0)
    def _():
        send_w0.wait_send()

    @pl.when(t < NT - 1)
    def _():
        send_v2.wait_send()
        forward.wait_send()

    @pl.when(jnp.logical_not(k_self))
    def _():
        send_k.wait_send()

    def end_r(j):
        own, copy, local = send_r(j)

        @pl.when(jnp.logical_not(own))
        def _():
            copy.wait_send()

    loop(SLABS, end_r)

    @pl.when(is_worker)
    def _():
        for dj in (-1, 0, 1):
            j = s + dj

            @pl.when((block < NT // BLOCK - 1) & (j >= 0) & (j < SLABS))
            def _(dj=dj):
                hand(dj).wait_send()

        def end_spread(h):
            def one(to):
                own, copy, local = spread(h, to)

                @pl.when(jnp.logical_not(own))
                def _():
                    copy.wait_send()

            loop(SLABS, one)

        loop(BLOCK, end_spread)


def body(nodes, coefficients):
    dma = pltpu.SemaphoreType.DMA
    fine = (DEPTH, ROWS, COLS)
    rimmed = (DEPTH + 2, ROWS + 2 * RIM, COLS)
    coarse = (DEPTH, HALF, LANES)
    scratch = [
        (7,) + fine, rimmed, rimmed, rimmed, fine, fine, fine,
        (7, DEPTH, HALF + 2 * RIM, LANES), (DEPTH, HALF + 2 * RIM, LANES), coarse, coarse,
        (7, 32, WIN, LANES), (BLOCK, 32, WIN, LANES), (BLOCK + 1, 34, WIN, LANES), coarse, coarse,
    ]
    sems = [(3, 2), (3, 2), (2,), (2,), (1,), (1,), (8,), (8,), (3,), (3,), (8, 8), (1,), (1,), (1,)]
    return pl.pallas_call(
        kernel,
        out_shape=jax.ShapeDtypeStruct(nodes.shape, F32),
        in_specs=[pl.BlockSpec(memory_space=pltpu.VMEM)] * 2,
        out_specs=pl.BlockSpec(memory_space=pltpu.VMEM),
        scratch_shapes=[pltpu.VMEM(shape, F32) for shape in scratch]
        + [dma(shape) for shape in sems]
        + [pltpu.SemaphoreType.REGULAR],
        compiler_params=pltpu.CompilerParams(
            collective_id=0, has_side_effects=True, vmem_limit_bytes=48 * 1024 * 1024
        ),
        name="pfasst",
    )(nodes, coefficients)


def solution(mesh):
    return jax.shard_map(
        body,
        mesh=mesh,
        in_specs=(P("tm", None, "space", None, None), P(None, "space", None, None)),
        out_specs=P("tm", None, "space", None, None),
        check_vma=False,
    )
```

time: 1050 us -> 190 us (0.18)
  the two profiles are of different devices: /device:TPU:30 before, /device:TPU:120 now
where the time goes in v1:
time: 190 us; the launch traced here: 188 us
  Pallas kernels  184 us (97%)
  local copies, waits for them, and re-layouts  4.05 us (2%)
    pallas_call x1, Pallas kernels, body(): pl.pallas_call(kernel, out_shape=jax.ShapeDtypeStruct(nodes.shape, F32),...  184 us
    unnamed x5, local copies, waits for them, and re-layouts  4.05 us

profile of v1, /device:TPU:120, one launch (start us, length us, event | category | flops | bytes accessed | tf_op | source)
XLA Modules:
  0.0 188.5 jit_solution(5271585993600036528)
XLA Ops:
  0.0 0.0 copy-start
  0.0 1.5 copy-done
  1.5 0.0 copy-start.1
  1.5 1.4 copy-done.1
  2.9 184.4 %pfasst.1 = f32[1,3,4,128,256]{4,3,2,1,0:T(8,128)S(1)} custom-call(f32[1,3,4,128,256]{4,3,2,1,0:T(8,128)S(1)} %copy-done.1, bf16[7,4,128,256]{3,2,1,0:T(8,128)(2,1)S(1)} %copy-done), custom_call_target="tpu_custom_call" | custom-call | tf_op jit(solution)/shard_map/pfasst/pallas_call | solution.py:548
  187.3 1.1 copy.4
Async XLA Ops:
  0.0 1.5 copy-start
  1.5 1.4 copy-start.1

commit v2 on v1

--- a/solution.py
+++ b/solution.py
@@ -9,7 +9,6 @@
 
 MESH = pl.DeviceIdType.MESH
 F32 = jnp.float32
-HIGH = lax.Precision.HIGHEST
 
 A0, A1, A2 = 0.2 * 5.0 / 24.0, 0.2 / 3.0, -0.2 / 24.0
 B0, B1, B2 = -0.2 / 24.0, 0.2 / 3.0, 0.2 * 5.0 / 24.0
@@ -24,10 +23,12 @@
 RIM = 8
 STRIP = 32
 WIN = 24
-
-
-def worker_place(j):
-    return 6 - 6 * lax.rem(j, 2)
+DEEP = 24
+
+
+def worker(half, j):
+    odd = lax.rem(j, 2)
+    return jnp.where(half == 0, 6 - 2 * odd, 2 * odd), j - odd + half
 
 
 def neighbours(value, axis, size, mask_low, mask_high):
@@ -60,17 +61,14 @@
 def pair_matrix(shape, long_axis, value):
     long = lax.broadcasted_iota(jnp.int32, shape, long_axis)
     short = lax.broadcasted_iota(jnp.int32, shape, 1 - long_axis)
-    return jnp.where((long == 2 * short) | (long == 2 * short + 1), value, 0.0).astype(F32)
-
-
-def restrict(plane):
-    across = jnp.dot(plane, pair_matrix((COLS, LANES), 0, 0.5), precision=HIGH, preferred_element_type=F32)
-    return jnp.dot(pair_matrix((HALF, ROWS), 1, 0.5), across, precision=HIGH, preferred_element_type=F32)
-
-
-def prolong(plane):
-    along = jnp.dot(pair_matrix((ROWS, HALF), 0, 1.0), plane, precision=HIGH, preferred_element_type=F32)
-    return jnp.dot(along, pair_matrix((LANES, COLS), 1, 1.0), precision=HIGH, preferred_element_type=F32)
+    return jnp.where((long == 2 * short) | (long == 2 * short + 1), value, 0.0).astype(jnp.bfloat16)
+
+
+def times(value, matrix):
+    high = value.astype(jnp.bfloat16)
+    low = (value - high.astype(F32)).astype(jnp.bfloat16)
+    dot = functools.partial(jnp.dot, preferred_element_type=F32)
+    return dot(high, matrix) + dot(low, matrix)
 
 
 def loop(count, fn, unroll=1):
@@ -83,7 +81,7 @@
 
 def kernel(
     nodes, coeffs, out,
-    kf, ab, bb, cb, v1, v2, v2p, kcp, rp, w0, wn, kb, rb, hb, ec, en,
+    kf, ab, bb, cb, v1, v2, v2p, kcp, rp, w0, wn, kb, rb, hb, ec, en, pairs, wide, narrow,
     halo_s, halo_r, shift_s, shift_r, k_s, k_r, r_s, r_r, hand_s, hand_r, e_s, e_r, f_s, f_r, known,
 ):
     t = lax.axis_index("tm")
@@ -91,7 +89,11 @@
     block = lax.div(t, BLOCK)
     place = lax.rem(t, BLOCK)
     base = block * BLOCK
-    is_worker = place == worker_place(s)
+    half = lax.rem(s, 2)
+    turn = jnp.where(half == 0, 6 - place, place)
+    is_worker = (turn == 0) | (turn == 2)
+    chunk = s - half + lax.div(turn, 2)
+    last_block = NT // BLOCK - 1
     strips = ROWS // STRIP
 
     def tell(sem, tm, sp):
@@ -115,11 +117,13 @@
         tell(barrier, t - 1, s)
 
     for dj in (-1, 0, 1):
-        j = s + dj
+        j = chunk + dj
 
         @pl.when(is_worker & (block > 0) & (j >= 0) & (j < SLABS))
         def _(j=j):
-            tell(barrier, base - BLOCK + worker_place(j), j)
+            for z in (0, 1):
+                to, at = worker(z, j)
+                tell(barrier, base - BLOCK + to, at)
 
     for buf in (ab, bb, cb):
         buf[:, 0:RIM, :] = jnp.zeros((DEPTH + 2, RIM, COLS), F32)
@@ -149,8 +153,8 @@
     loop(strips, lambda i: combine_a(3, i))
 
     expect = 14 + jnp.where(cross_up, 1, 0) + jnp.where(cross_down, 1, 0)
-    hands = 3 - jnp.where(s == 0, 1, 0) - jnp.where(s == SLABS - 1, 1, 0)
-    expect = expect + jnp.where(is_worker & (block < NT // BLOCK - 1), hands, 0)
+    hands = 6 - jnp.where(chunk == 0, 2, 0) - jnp.where(chunk == SLABS - 1, 2, 0)
+    expect = expect + jnp.where(is_worker & (block < last_block), hands, 0)
     pl.semaphore_wait(barrier, expect)
 
     inner = pl.ds(RIM, ROWS)
@@ -180,6 +184,21 @@
     for n in range(1, BLOCK):
         tell(known, base + lax.rem(place + n, BLOCK), s)
 
+    narrow[...] = pair_matrix((COLS, LANES), 0, 0.25)
+    wide[...] = pair_matrix((LANES, COLS), 1, 1.0)
+
+    def restrict(p, across):
+        pairs[p] = across
+        return pairs[p, pl.ds(0, HALF, stride=2), :] + pairs[p, pl.ds(1, HALF, stride=2), :]
+
+    def average(p, value):
+        return restrict(p, times(value, narrow[...]))
+
+    def prolong(p, value):
+        pairs[p, pl.ds(0, HALF, stride=2), :] = value
+        pairs[p, pl.ds(1, HALF, stride=2), :] = value
+        return times(pairs[p], wide[...])
+
     def shift(src, dst, n, tm):
         return pltpu.make_async_remote_copy(
             src_ref=src, dst_ref=dst, send_sem=shift_s.at[n], recv_sem=shift_r.at[n],
@@ -189,10 +208,8 @@
     send_w0 = shift(w0, wn, 0, t - 1)
     send_v2 = shift(v2, v2p, 1, t + 1)
 
-    def start_coarse(p):
-        w0[p] = restrict(nodes[0, 0, p])
-
-    loop(DEPTH, start_coarse)
+    for p in range(DEPTH):
+        w0[p] = average(p, nodes[0, 0, p])
 
     @pl.when(t > 0)
     def _():
@@ -251,12 +268,12 @@
         for p in which:
             loop(strips, lambda i, p=p: fn(p, i))
 
-    def coarse_weights(n):
-        m, p = lax.div(n, DEPTH), lax.rem(n, DEPTH)
-        plane = coeffs[m, p].astype(F32)
-        kcp[m, p, RIM : RIM + HALF, :] = restrict(plane)
-
-    loop(7 * DEPTH, coarse_weights)
+    def coarse_weights(m):
+        for p in range(DEPTH):
+            across = jnp.dot(coeffs[m, p], narrow[...], preferred_element_type=F32)
+            kcp[m, p, RIM : RIM + HALF, :] = restrict(p, across)
+
+    loop(7, coarse_weights)
 
     def scale_weights(p):
         here = slice(RIM, RIM + HALF)
@@ -271,22 +288,37 @@
     planes(first_node, (1, 2))
     pl.semaphore_wait(known, BLOCK - 1)
 
-    goal = worker_place(place)
-    k_self = (goal == place) & (place == s)
     window = pl.ds(pl.multiple_of(8 * place, 8), WIN)
-    slab = pl.ds(pl.multiple_of(DEPTH * s, DEPTH), DEPTH)
-    send_k = pltpu.make_async_remote_copy(
-        src_ref=kcp.at[:, :, window], dst_ref=kb.at[:, slab], send_sem=k_s.at[0], recv_sem=k_r.at[0],
-        device_id=(base + goal, place), device_id_type=MESH,
-    )
-
-    @pl.when(k_self)
-    def _():
-        pltpu.make_async_copy(kcp.at[:, :, window], kb.at[:, slab], k_r.at[0]).start()
-
-    @pl.when(jnp.logical_not(k_self))
-    def _():
-        send_k.start()
+
+    def send_k(z):
+        to, at = worker(z, place)
+        src, dst = kcp.at[:, :, window], kb.at[:, pl.ds(DEPTH * s - 8 * z, DEPTH)]
+        own = (to == place) & (at == s)
+        needed = s >= 2 if z else s <= 5
+        copy = pltpu.make_async_remote_copy(
+            src_ref=src, dst_ref=dst, send_sem=k_s.at[z], recv_sem=k_r.at[0],
+            device_id=(base + to, at), device_id_type=MESH,
+        )
+        return needed & own, needed & jnp.logical_not(own), copy, pltpu.make_async_copy(src, dst, k_r.at[0])
+
+    def start(parts):
+        own, other, copy, local = parts
+
+        @pl.when(own)
+        def _():
+            local.start()
+
+        @pl.when(other)
+        def _():
+            copy.start()
+
+    def end(parts):
+        @pl.when(parts[1])
+        def _():
+            parts[2].wait_send()
+
+    for z in (0, 1):
+        start(send_k(z))
 
     take_halo(ab, 0, True)
     planes(first_node, (0,))
@@ -316,140 +348,149 @@
     def _():
         send_w0.wait_recv()
 
-    def right_side(p):
-        rp[p, RIM : RIM + HALF, :] = restrict(out[0, 0, p]) - wn[p]
-
-    loop(DEPTH, right_side)
-
-    def send_r(j):
-        to = worker_place(j)
-        rows = pl.ds(pl.multiple_of(8 * j, 8), WIN)
-        own = (to == place) & (j == s)
+    for p in range(DEPTH):
+        rp[p, RIM : RIM + HALF, :] = average(p, out[0, 0, p]) - wn[p]
+
+    def send_r(z, j):
+        to, at = worker(z, j)
+        src = rp.at[:, pl.ds(pl.multiple_of(8 * j, 8), WIN)]
+        dst = rb.at[place, pl.ds(DEPTH * s - 8 * z, DEPTH)]
+        own = (to == place) & (at == s)
+        needed = DEPTH * s + 3 >= 9 + place if z else DEPTH * s < 23 - place
         copy = pltpu.make_async_remote_copy(
-            src_ref=rp.at[:, rows], dst_ref=rb.at[place, slab], send_sem=r_s.at[j], recv_sem=r_r.at[place],
-            device_id=(base + to, j), device_id_type=MESH,
-        )
-        return own, copy, pltpu.make_async_copy(rp.at[:, rows], rb.at[place, slab], r_r.at[place])
-
-    def start_r(j):
-        own, copy, local = send_r(j)
-
-        @pl.when(own)
-        def _():
-            local.start()
-
-        @pl.when(jnp.logical_not(own))
-        def _():
-            copy.start()
-
-    loop(SLABS, start_r)
+            src_ref=src, dst_ref=dst, send_sem=r_s.at[z, j], recv_sem=r_r.at[place, s],
+            device_id=(base + to, at), device_id_type=MESH,
+        )
+        return needed & own, needed & jnp.logical_not(own), copy, pltpu.make_async_copy(src, dst, r_r.at[place, s])
+
+    for z in (0, 1):
+        loop(SLABS, lambda j, z=z: start(send_r(z, j)))
 
     @pl.when(t > 0)
     def _():
         send_v2.wait_recv()
 
-    def early(p):
-        @pl.when(t > 0)
-        def _():
-            out[0, 0, p] = v2p[p] + prolong(restrict(nodes[0, 0, p] - v2p[p]))
-
-        @pl.when(t == 0)
-        def _():
-            out[0, 0, p] = nodes[0, 0, p]
-
-        gap = prolong(wn[p] - restrict(v2[p]))
+    @pl.when(t > 0)
+    def _():
+        for p in range(DEPTH):
+            out[0, 0, p] = v2p[p] + prolong(p, average(p, nodes[0, 0, p] - v2p[p]))
+
+    @pl.when(t == 0)
+    def _():
+        out[0, 0] = nodes[0, 0]
+
+    for p in range(DEPTH):
+        gap = prolong(p, wn[p] - average(p, v2[p]))
         out[0, 1, p] = v1[p] + 0.5 * gap
         out[0, 2, p] = v2[p] + gap
 
-    loop(DEPTH, early)
-
-    def hand(dj):
-        j = s + dj
+    def hand(z, dj):
+        count = 8 if z else 16
+        source = 9 if z else 1 + 8 * half
+        target = jnp.where(half == 0, 1, 17) if z else source
+        to, at = worker(1 - half if z else half, chunk + dj)
         return pltpu.make_async_remote_copy(
-            src_ref=hb.at[BLOCK, pl.ds(1, 32), pl.ds(8, 8)],
-            dst_ref=hb.at[0, pl.ds(1, 32), pl.ds(8 - 8 * dj, 8)],
-            send_sem=hand_s.at[dj + 1],
-            recv_sem=hand_r.at[dj + 1],
-            device_id=(base + BLOCK + worker_place(j), j),
+            src_ref=hb.at[BLOCK, pl.ds(source, count), pl.ds(8, 8)],
+            dst_ref=hb.at[0, pl.ds(target, count), pl.ds(8 - 8 * dj, 8)],
+            send_sem=hand_s.at[z, dj + 1],
+            recv_sem=hand_r.at[z, dj + 1],
+            device_id=(base + BLOCK + to, at),
             device_id_type=MESH,
         )
 
-    def spread(h, to):
-        src = hb.at[h + 1, pl.ds(1 + DEPTH * to, DEPTH), pl.ds(8, 8)]
-        dst = en.at[:, pl.ds(pl.multiple_of(8 * s, 8), 8)]
+    def spread(h, n):
+        to = 4 * half + n
+        src = hb.at[h + 1, pl.ds(1 + 8 * half + DEPTH * n, DEPTH), pl.ds(8, 8)]
+        dst = en.at[:, pl.ds(pl.multiple_of(8 * chunk, 8), 8)]
         own = (h == place) & (to == s)
         copy = pltpu.make_async_remote_copy(
-            src_ref=src, dst_ref=dst, send_sem=e_s.at[h, to], recv_sem=e_r.at[0],
+            src_ref=src, dst_ref=dst, send_sem=e_s.at[h, n], recv_sem=e_r.at[0],
             device_id=(base + h, to), device_id_type=MESH,
         )
-        return own, copy, pltpu.make_async_copy(src, dst, e_r.at[0])
+        return own, jnp.logical_not(own), copy, pltpu.make_async_copy(src, dst, e_r.at[0])
 
     def start_spread(h):
-        def one(to):
-            own, copy, local = spread(h, to)
-
-            @pl.when(own)
-            def _():
-                local.start()
-
-            @pl.when(jnp.logical_not(own))
-            def _():
-                copy.start()
-
-        loop(SLABS, one)
+        loop(4, lambda n: start(spread(h, n)))
 
     @pl.when(is_worker)
     def _():
         def clear(h):
             hb[h, 0] = jnp.zeros((WIN, LANES), F32)
-            hb[h, 33] = jnp.zeros((WIN, LANES), F32)
+            hb[h, DEEP + 1] = jnp.zeros((WIN, LANES), F32)
 
         loop(BLOCK + 1, clear)
 
         @pl.when(block == 0)
         def _():
-            hb[0, 1:33] = jnp.zeros((32, WIN, LANES), F32)
-
-        @pl.when((block > 0) & (s == 0))
-        def _():
-            hb[0, 1:33, 0:8, :] = jnp.zeros((32, 8, LANES), F32)
-
-        @pl.when((block > 0) & (s == SLABS - 1))
-        def _():
-            hb[0, 1:33, 16:24, :] = jnp.zeros((32, 8, LANES), F32)
+            hb[0, 1 : DEEP + 1] = jnp.zeros((DEEP, WIN, LANES), F32)
+
+        @pl.when((block > 0) & (chunk == 0))
+        def _():
+            hb[0, 1 : DEEP + 1, 0:8, :] = jnp.zeros((DEEP, 8, LANES), F32)
+
+        @pl.when((block > 0) & (chunk == SLABS - 1))
+        def _():
+            hb[0, 1 : DEEP + 1, 16:24, :] = jnp.zeros((DEEP, 8, LANES), F32)
 
         pltpu.make_async_copy(kb, kb, k_r.at[0]).wait()
         for dj in (-1, 0, 1):
-            @pl.when((block > 0) & (s - dj >= 0) & (s - dj < SLABS))
+            @pl.when((block > 0) & (chunk - dj >= 0) & (chunk - dj < SLABS))
             def _(dj=dj):
-                hand(dj).wait_recv()
+                hand(0, dj).wait_recv()
+                hand(1, dj).wait_recv()
+
+        lane = lax.broadcasted_iota(jnp.int32, (WIN, LANES), 1)
+        first, last = lane == 0, lane == LANES - 1
+
+        def slopes(v):
+            right, left = neighbours(v, 1, LANES, first, last)
+            down, up = rows_around(v, WIN)
+            over_y = right - left
+            s_down, s_up = rows_around(over_y, WIN)
+            return v, over_y, down - up, right + left, down + up, s_down - s_up
 
         def advance(h):
-            pltpu.make_async_copy(rb.at[h], rb.at[h], r_r.at[h]).wait()
-
-            def plane(p):
-                value = stencil(
-                    hb[h, p], hb[h, p + 1], hb[h, p + 2],
-                    [kb[m, p] for m in range(7)], WIN, LANES, 0, WIN,
-                )
-                hb[h + 1, p + 1] = value + rb[h, p]
-
-            loop(32, plane, unroll=2)
-
-            @pl.when(block == NT // BLOCK - 1)
+            count = lax.div(26 - h, 4)
+            slab0 = half * (SLABS - count)
+            start_plane = DEPTH * slab0 - 8 * half
+
+            def arrived(i):
+                part = rb.at[h, pl.ds(start_plane + DEPTH * i, DEPTH)]
+                pltpu.make_async_copy(part, part, r_r.at[h, slab0 + i]).wait()
+
+            loop(count, arrived)
+            low, low_y, low_x = slopes(hb[h, start_plane])[:3]
+
+            def group(i, carry):
+                (low, low_y, low_x), here = carry
+                for n in range(DEPTH):
+                    p = start_plane + DEPTH * i + n
+                    above = slopes(hb[h, p + 2])
+                    v, v_y, v_x, around_y, around_x, v_xy = here
+                    total = rb[h, p] + kb[0, p] * (above[0] + low) + kb[1, p] * around_x + kb[2, p] * around_y
+                    total = total + kb[3, p] * (above[2] - low_x) + kb[4, p] * (above[1] - low_y)
+                    hb[h + 1, p + 1] = total + kb[5, p] * v_xy + kb[6, p] * v
+                    low, low_y, low_x = v, v_y, v_x
+                    here = above
+                return (low, low_y, low_x), here
+
+            lax.fori_loop(0, count, group, ((low, low_y, low_x), slopes(hb[h, start_plane + 1])))
+
+            @pl.when(block == last_block)
             def _():
                 start_spread(h)
 
         loop(BLOCK, advance)
 
-        @pl.when(block < NT // BLOCK - 1)
+        @pl.when(block < last_block)
         def _():
             for dj in (-1, 0, 1):
-                j = s + dj
+                j = chunk + dj
 
                 @pl.when((j >= 0) & (j < SLABS))
                 def _(dj=dj):
-                    hand(dj).start()
+                    hand(0, dj).start()
+                    hand(1, dj).start()
 
             loop(BLOCK, start_spread)
 
@@ -462,23 +503,19 @@
     def _():
         forward.start()
 
-    def end_node(p):
-        gain = prolong(en[p])
+    for p in range(DEPTH):
+        gain = prolong(p, en[p])
         out[0, 2, p] += gain
         out[0, 1, p] += 0.5 * gain
 
-    loop(DEPTH, end_node)
-
     @pl.when(t > 0)
     def _():
         forward.wait_recv()
 
-        def start_node(p):
-            gain = prolong(ec[p])
+        for p in range(DEPTH):
+            gain = prolong(p, ec[p])
             out[0, 0, p] += gain
             out[0, 1, p] += 0.5 * gain
-
-        loop(DEPTH, start_node)
 
     for phase, buf in enumerate((ab, bb, cb)):
 
@@ -499,37 +536,22 @@
         send_v2.wait_send()
         forward.wait_send()
 
-    @pl.when(jnp.logical_not(k_self))
-    def _():
-        send_k.wait_send()
-
-    def end_r(j):
-        own, copy, local = send_r(j)
-
-        @pl.when(jnp.logical_not(own))
-        def _():
-            copy.wait_send()
-
-    loop(SLABS, end_r)
+    for z in (0, 1):
+        end(send_k(z))
+        loop(SLABS, lambda j, z=z: end(send_r(z, j)))
 
     @pl.when(is_worker)
     def _():
         for dj in (-1, 0, 1):
-            j = s + dj
-
-            @pl.when((block < NT // BLOCK - 1) & (j >= 0) & (j < SLABS))
+            j = chunk + dj
+
+            @pl.when((block < last_block) & (j >= 0) & (j < SLABS))
             def _(dj=dj):
-                hand(dj).wait_send()
+                hand(0, dj).wait_send()
+                hand(1, dj).wait_send()
 
         def end_spread(h):
-            def one(to):
-                own, copy, local = spread(h, to)
-
-                @pl.when(jnp.logical_not(own))
-                def _():
-                    copy.wait_send()
-
-            loop(SLABS, one)
+            loop(4, lambda n: end(spread(h, n)))
 
         loop(BLOCK, end_spread)
 
@@ -542,15 +564,17 @@
     scratch = [
         (7,) + fine, rimmed, rimmed, rimmed, fine, fine, fine,
         (7, DEPTH, HALF + 2 * RIM, LANES), (DEPTH, HALF + 2 * RIM, LANES), coarse, coarse,
-        (7, 32, WIN, LANES), (BLOCK, 32, WIN, LANES), (BLOCK + 1, 34, WIN, LANES), coarse, coarse,
+        (7, DEEP, WIN, LANES), (BLOCK, DEEP, WIN, LANES), (BLOCK + 1, DEEP + 2, WIN, LANES), coarse, coarse,
+        (DEPTH, ROWS, LANES),
     ]
-    sems = [(3, 2), (3, 2), (2,), (2,), (1,), (1,), (8,), (8,), (3,), (3,), (8, 8), (1,), (1,), (1,)]
+    sems = [(3, 2), (3, 2), (2,), (2,), (2,), (1,), (2, 8), (8, 8), (2, 3), (2, 3), (8, 4), (1,), (1,), (1,)]
     return pl.pallas_call(
         kernel,
         out_shape=jax.ShapeDtypeStruct(nodes.shape, F32),
         in_specs=[pl.BlockSpec(memory_space=pltpu.VMEM)] * 2,
         out_specs=pl.BlockSpec(memory_space=pltpu.VMEM),
         scratch_shapes=[pltpu.VMEM(shape, F32) for shape in scratch]
+        + [pltpu.VMEM((LANES, COLS), jnp.bfloat16), pltpu.VMEM((COLS, LANES), jnp.bfloat16)]
         + [dma(shape) for shape in sems]
         + [pltpu.SemaphoreType.REGULAR],
         compiler_params=pltpu.CompilerParams(

time: 190 us -> 165 us (0.87)
  Pallas kernels: 184 us -> 161 us
    pallas_call x1, Pallas kernels: 184 us -> 161 us  [body(): pl.pallas_call(kernel, out_shape=jax.ShapeDtypeStruct(nodes.shape, F32),...]
where the time goes in v2:
time: 165 us
  Pallas kernels  161 us (98%)
  local copies, waits for them, and re-layouts  4.05 us (2%)
    pallas_call x1, Pallas kernels, body(): pl.pallas_call(kernel, out_shape=jax.ShapeDtypeStruct(nodes.shape, F32),...  161 us
    unnamed x5, local copies, waits for them, and re-layouts  4.05 us

profile of v2, /device:TPU:120, one launch (start us, length us, event | category | flops | bytes accessed | tf_op | source)
XLA Modules:
  0.0 164.8 jit_solution(5500736879958891145)
XLA Ops:
  0.0 0.0 copy-start
  0.0 1.5 copy-done
  1.5 0.0 copy-start.1
  1.5 1.4 copy-done.1
  2.9 160.8 %pfasst.1 = f32[1,3,4,128,256]{4,3,2,1,0:T(8,128)S(1)} custom-call(f32[1,3,4,128,256]{4,3,2,1,0:T(8,128)S(1)} %copy-done.1, bf16[7,4,128,256]{3,2,1,0:T(8,128)(2,1)S(1)} %copy-done), custom_call_target="tpu_custom_call" | custom-call | tf_op jit(solution)/shard_map/pfasst/pallas_call | solution.py:571
  163.7 1.1 copy.4
Async XLA Ops:
  0.0 1.5 copy-start
  1.5 1.4 copy-start.1

commit v3 on v2

--- a/solution.py
+++ b/solution.py
@@ -28,7 +28,7 @@
 
 def worker(half, j):
     odd = lax.rem(j, 2)
-    return jnp.where(half == 0, 6 - 2 * odd, 2 * odd), j - odd + half
+    return 2 * lax.rem(j, 4), 2 * jnp.where(half == 0, odd, 3 - odd) + lax.div(j, 4)
 
 
 def neighbours(value, axis, size, mask_low, mask_high):
@@ -89,10 +89,10 @@
     block = lax.div(t, BLOCK)
     place = lax.rem(t, BLOCK)
     base = block * BLOCK
-    half = lax.rem(s, 2)
-    turn = jnp.where(half == 0, 6 - place, place)
-    is_worker = (turn == 0) | (turn == 2)
-    chunk = s - half + lax.div(turn, 2)
+    half = lax.div(s, 4)
+    chunk = 4 * lax.rem(s, 2) + lax.div(place, 2)
+    odd = lax.rem(lax.div(s, 2), 2)
+    is_worker = (lax.rem(place, 2) == 0) & (lax.rem(chunk, 2) == jnp.where(half == 0, odd, 1 - odd))
     last_block = NT // BLOCK - 1
     strips = ROWS // STRIP
 

time: 165 us -> 144 us (0.87)
  Pallas kernels: 161 us -> 139 us
    pallas_call x1, Pallas kernels: 161 us -> 139 us  [body(): pl.pallas_call(kernel, out_shape=jax.ShapeDtypeStruct(nodes.shape, F32),...]
where the time goes in v3:
time: 144 us; the launch traced here: 143 us
  Pallas kernels  139 us (97%)
  local copies, waits for them, and re-layouts  4.05 us (3%)
    pallas_call x1, Pallas kernels, body(): pl.pallas_call(kernel, out_shape=jax.ShapeDtypeStruct(nodes.shape, F32),...  139 us
    unnamed x5, local copies, waits for them, and re-layouts  4.05 us

profile of v3, /device:TPU:120, one launch (start us, length us, event | category | flops | bytes accessed | tf_op | source)
XLA Modules:
  0.0 143.3 jit_solution(4526110465145675647)
XLA Ops:
  0.0 0.0 copy-start
  0.0 1.5 %copy-done = bf16[7,4,128,256]{3,2,1,0:T(8,128)(2,1)S(1)} copy-done((bf16[7,4,128,256]{3,2,1,0:T(8,128)(2,1)S(1)}, bf16[7,4,128,256]{3,2,1,0:T(8,128)(2,1)}, u32[]{:S(2)}) %copy-start) | copy-done | bytes 1835032
  1.5 0.0 copy-start.1
  1.5 1.4 copy-done.1
  2.9 139.2 %pfasst.1 = f32[1,3,4,128,256]{4,3,2,1,0:T(8,128)S(1)} custom-call(f32[1,3,4,128,256]{4,3,2,1,0:T(8,128)S(1)} %copy-done.1, bf16[7,4,128,256]{3,2,1,0:T(8,128)(2,1)S(1)} %copy-done), custom_call_target="tpu_custom_call" | custom-call | tf_op jit(solution)/shard_map/pfasst/pallas_call | solution.py:571
  142.1 1.1 copy.4
Async XLA Ops:
  0.0 1.5 %copy-start = (bf16[7,4,128,256]{3,2,1,0:T(8,128)(2,1)S(1)}, bf16[7,4,128,256]{3,2,1,0:T(8,128)(2,1)}, u32[]{:S(2)}) copy-start(bf16[7,4,128,256]{3,2,1,0:T(8,128)(2,1)} %coeffs.1) | copy-start | bytes 5505028
  1.5 1.4 copy-start.1

commit v4 on v3

--- a/solution.py
+++ b/solution.py
@@ -80,9 +80,9 @@
 
 
 def kernel(
-    nodes, coeffs, out,
-    kf, ab, bb, cb, v1, v2, v2p, kcp, rp, w0, wn, kb, rb, hb, ec, en, pairs, wide, narrow,
-    halo_s, halo_r, shift_s, shift_r, k_s, k_r, r_s, r_r, hand_s, hand_r, e_s, e_r, f_s, f_r, known,
+    nodes_hbm, coeffs_hbm, out,
+    nodes, coeffs, kf, ab, bb, cb, v1, v2, v2p, kcp, rp, w0, wn, kb, rb, hb, ec, en, pairs, wide, narrow,
+    halo_s, halo_r, shift_s, shift_r, k_s, k_r, r_s, r_r, hand_s, hand_r, e_s, e_r, f_s, f_r, in_s, kf_s, kf_r, known,
 ):
     t = lax.axis_index("tm")
     s = lax.axis_index("space")
@@ -99,6 +99,11 @@
     def tell(sem, tm, sp):
         pl.semaphore_signal(sem, inc=1, device_id=(tm, sp), device_id_type=MESH)
 
+    load_nodes = pltpu.make_async_copy(nodes_hbm, nodes, in_s.at[0])
+    load_coeffs = pltpu.make_async_copy(coeffs_hbm, coeffs, in_s.at[1])
+    load_nodes.start()
+    load_coeffs.start()
+
     barrier = pltpu.get_barrier_semaphore()
     for n in range(1, SLABS):
         tell(barrier, t, lax.rem(s + n, SLABS))
@@ -116,6 +121,11 @@
     def _():
         tell(barrier, t - 1, s)
 
+    @pl.when(is_worker)
+    def _():
+        for n in range(1, NT // BLOCK):
+            tell(barrier, lax.rem(t + BLOCK * n, NT), s)
+
     for dj in (-1, 0, 1):
         j = chunk + dj
 
@@ -139,8 +149,8 @@
         for buf in (ab, bb, cb):
             buf[DEPTH + 1, RIM : RIM + ROWS, :] = jnp.zeros((ROWS, COLS), F32)
 
-    kcp[:, :, 0:RIM, :] = jnp.zeros((7, DEPTH, RIM, LANES), F32)
-    kcp[:, :, RIM + HALF :, :] = jnp.zeros((7, DEPTH, RIM, LANES), F32)
+    kcp[:, 0:RIM, :] = jnp.zeros((7, RIM, LANES), F32)
+    kcp[:, RIM + HALF :, :] = jnp.zeros((7, RIM, LANES), F32)
     rp[:, 0:RIM, :] = jnp.zeros((DEPTH, RIM, LANES), F32)
     rp[:, RIM + HALF :, :] = jnp.zeros((DEPTH, RIM, LANES), F32)
 
@@ -149,12 +159,14 @@
         there = pl.ds(pl.multiple_of(RIM + i * STRIP, 8), STRIP)
         ab[p + 1, there, :] = A0 * nodes[0, 0, p, here, :] + A1 * nodes[0, 1, p, here, :] + A2 * nodes[0, 2, p, here, :]
 
+    load_nodes.wait()
     loop(strips, lambda i: combine_a(0, i))
     loop(strips, lambda i: combine_a(3, i))
+    load_coeffs.wait()
 
     expect = 14 + jnp.where(cross_up, 1, 0) + jnp.where(cross_down, 1, 0)
     hands = 6 - jnp.where(chunk == 0, 2, 0) - jnp.where(chunk == SLABS - 1, 2, 0)
-    expect = expect + jnp.where(is_worker & (block < last_block), hands, 0)
+    expect = expect + jnp.where(is_worker, last_block, 0) + jnp.where(is_worker & (block < last_block), hands, 0)
     pl.semaphore_wait(barrier, expect)
 
     inner = pl.ds(RIM, ROWS)
@@ -268,23 +280,16 @@
         for p in which:
             loop(strips, lambda i, p=p: fn(p, i))
 
-    def coarse_weights(m):
-        for p in range(DEPTH):
-            across = jnp.dot(coeffs[m, p], narrow[...], preferred_element_type=F32)
-            kcp[m, p, RIM : RIM + HALF, :] = restrict(p, across)
-
-    loop(7, coarse_weights)
-
-    def scale_weights(p):
-        here = slice(RIM, RIM + HALF)
-        k = [kcp[m, p, here, :] for m in range(7)]
-        kcp[0, p, here, :] = 0.2 * k[0]
-        for m in range(1, 5):
-            kcp[m, p, here, :] = 0.05 * k[m]
-        kcp[5, p, here, :] = 0.025 * k[5]
-        kcp[6, p, here, :] = 1.0 - (0.4 * k[0] + 0.1 * (k[1] + k[2]) + 0.2 * k[6])
-
-    loop(DEPTH, scale_weights)
+    inside = slice(RIM, RIM + HALF)
+    k = []
+    for m in range(7):
+        across = jnp.dot(coeffs[m, block], narrow[...], preferred_element_type=F32)
+        k.append(restrict(m % DEPTH, across))
+    kcp[0, inside, :] = 0.2 * k[0]
+    for m in range(1, 5):
+        kcp[m, inside, :] = 0.05 * k[m]
+    kcp[5, inside, :] = 0.025 * k[5]
+    kcp[6, inside, :] = 1.0 - (0.4 * k[0] + 0.1 * (k[1] + k[2]) + 0.2 * k[6])
     planes(first_node, (1, 2))
     pl.semaphore_wait(known, BLOCK - 1)
 
@@ -292,7 +297,7 @@
 
     def send_k(z):
         to, at = worker(z, place)
-        src, dst = kcp.at[:, :, window], kb.at[:, pl.ds(DEPTH * s - 8 * z, DEPTH)]
+        src, dst = kcp.at[:, window], kb.at[:, s - 2 * z, block]
         own = (to == place) & (at == s)
         needed = s >= 2 if z else s <= 5
         copy = pltpu.make_async_remote_copy(
@@ -319,6 +324,13 @@
 
     for z in (0, 1):
         start(send_k(z))
+
+    def pass_k(n):
+        part = kb.at[:, :, block]
+        return pltpu.make_async_remote_copy(
+            src_ref=part, dst_ref=part, send_sem=kf_s.at[n - 1], recv_sem=kf_r.at[block],
+            device_id=(lax.rem(t + BLOCK * n, NT), s), device_id_type=MESH,
+        )
 
     take_halo(ab, 0, True)
     planes(first_node, (0,))
@@ -334,7 +346,16 @@
     planes(last_node, (3,))
     send_halo(cb, 2, True)
 
-    @pl.when(t < NT - 1)
+    @pl.when(is_worker)
+    def _():
+        part = kb.at[:, :, block]
+        pltpu.make_async_copy(part, part, k_r.at[0]).wait()
+        for n in range(1, NT // BLOCK):
+            pass_k(n).start()
+
+    on_chip = lax.rem(place, 2) == 0
+
+    @pl.when(on_chip)
     def _():
         send_v2.start()
 
@@ -366,23 +387,32 @@
     for z in (0, 1):
         loop(SLABS, lambda j, z=z: start(send_r(z, j)))
 
-    @pl.when(t > 0)
-    def _():
-        send_v2.wait_recv()
-
-    @pl.when(t > 0)
-    def _():
-        for p in range(DEPTH):
-            out[0, 0, p] = v2p[p] + prolong(p, average(p, nodes[0, 0, p] - v2p[p]))
-
-    @pl.when(t == 0)
-    def _():
-        out[0, 0] = nodes[0, 0]
+    @pl.when(jnp.logical_not(on_chip))
+    def _():
+        for z in (0, 1):
+            loop(SLABS, lambda j, z=z: end(send_r(z, j)))
+
+        @pl.when(t < NT - 1)
+        def _():
+            send_v2.start()
+
+    def early_start():
+        @pl.when(t > 0)
+        def _():
+            send_v2.wait_recv()
+            for p in range(DEPTH):
+                out[0, 0, p] = v2p[p] + prolong(p, average(p, nodes[0, 0, p] - v2p[p]))
+
+        @pl.when(t == 0)
+        def _():
+            out[0, 0] = nodes[0, 0]
 
     for p in range(DEPTH):
         gap = prolong(p, wn[p] - average(p, v2[p]))
         out[0, 1, p] = v1[p] + 0.5 * gap
         out[0, 2, p] = v2[p] + gap
+
+    pl.when(jnp.logical_not(is_worker))(early_start)
 
     def hand(z, dj):
         count = 8 if z else 16
@@ -432,7 +462,10 @@
         def _():
             hb[0, 1 : DEEP + 1, 16:24, :] = jnp.zeros((DEEP, 8, LANES), F32)
 
-        pltpu.make_async_copy(kb, kb, k_r.at[0]).wait()
+        for n in range(1, NT // BLOCK):
+            other = lax.rem(block + n, NT // BLOCK)
+            part = kb.at[:, :, other]
+            pltpu.make_async_copy(part, part, kf_r.at[other]).wait()
         for dj in (-1, 0, 1):
             @pl.when((block > 0) & (chunk - dj >= 0) & (chunk - dj < SLABS))
             def _(dj=dj):
@@ -452,7 +485,8 @@
         def advance(h):
             count = lax.div(26 - h, 4)
             slab0 = half * (SLABS - count)
-            start_plane = DEPTH * slab0 - 8 * half
+            quad = slab0 - 2 * half
+            start_plane = DEPTH * quad
 
             def arrived(i):
                 part = rb.at[h, pl.ds(start_plane + DEPTH * i, DEPTH)]
@@ -467,9 +501,10 @@
                     p = start_plane + DEPTH * i + n
                     above = slopes(hb[h, p + 2])
                     v, v_y, v_x, around_y, around_x, v_xy = here
-                    total = rb[h, p] + kb[0, p] * (above[0] + low) + kb[1, p] * around_x + kb[2, p] * around_y
-                    total = total + kb[3, p] * (above[2] - low_x) + kb[4, p] * (above[1] - low_y)
-                    hb[h + 1, p + 1] = total + kb[5, p] * v_xy + kb[6, p] * v
+                    k = [kb[m, quad + i, n] for m in range(7)]
+                    total = rb[h, p] + k[0] * (above[0] + low) + k[1] * around_x + k[2] * around_y
+                    total = total + k[3] * (above[2] - low_x) + k[4] * (above[1] - low_y)
+                    hb[h + 1, p + 1] = total + k[5] * v_xy + k[6] * v
                     low, low_y, low_x = v, v_y, v_x
                     here = above
                 return (low, low_y, low_x), here
@@ -508,6 +543,8 @@
         out[0, 2, p] += gain
         out[0, 1, p] += 0.5 * gain
 
+    pl.when(is_worker)(early_start)
+
     @pl.when(t > 0)
     def _():
         forward.wait_recv()
@@ -538,10 +575,16 @@
 
     for z in (0, 1):
         end(send_k(z))
-        loop(SLABS, lambda j, z=z: end(send_r(z, j)))
+
+        @pl.when(on_chip)
+        def _(z=z):
+            loop(SLABS, lambda j: end(send_r(z, j)))
 
     @pl.when(is_worker)
     def _():
+        for n in range(1, NT // BLOCK):
+            pass_k(n).wait_send()
+
         for dj in (-1, 0, 1):
             j = chunk + dj
 
@@ -563,17 +606,18 @@
     coarse = (DEPTH, HALF, LANES)
     scratch = [
         (7,) + fine, rimmed, rimmed, rimmed, fine, fine, fine,
-        (7, DEPTH, HALF + 2 * RIM, LANES), (DEPTH, HALF + 2 * RIM, LANES), coarse, coarse,
-        (7, DEEP, WIN, LANES), (BLOCK, DEEP, WIN, LANES), (BLOCK + 1, DEEP + 2, WIN, LANES), coarse, coarse,
+        (7, HALF + 2 * RIM, LANES), (DEPTH, HALF + 2 * RIM, LANES), coarse, coarse,
+        (7, DEEP // DEPTH, DEPTH, WIN, LANES), (BLOCK, DEEP, WIN, LANES), (BLOCK + 1, DEEP + 2, WIN, LANES), coarse, coarse,
         (DEPTH, ROWS, LANES),
     ]
-    sems = [(3, 2), (3, 2), (2,), (2,), (2,), (1,), (2, 8), (8, 8), (2, 3), (2, 3), (8, 4), (1,), (1,), (1,)]
+    sems = [(3, 2), (3, 2), (2,), (2,), (2,), (1,), (2, 8), (8, 8), (2, 3), (2, 3), (8, 4), (1,), (1,), (1,), (2,), (3,), (4,)]
     return pl.pallas_call(
         kernel,
         out_shape=jax.ShapeDtypeStruct(nodes.shape, F32),
-        in_specs=[pl.BlockSpec(memory_space=pltpu.VMEM)] * 2,
+        in_specs=[pl.BlockSpec(memory_space=pltpu.HBM)] * 2,
         out_specs=pl.BlockSpec(memory_space=pltpu.VMEM),
-        scratch_shapes=[pltpu.VMEM(shape, F32) for shape in scratch]
+        scratch_shapes=[pltpu.VMEM(nodes.shape, F32), pltpu.VMEM(coefficients.shape, jnp.bfloat16)]
+        + [pltpu.VMEM(shape, F32) for shape in scratch]
         + [pltpu.VMEM((LANES, COLS), jnp.bfloat16), pltpu.VMEM((COLS, LANES), jnp.bfloat16)]
         + [dma(shape) for shape in sems]
         + [pltpu.SemaphoreType.REGULAR],

time: 144 us -> 128 us (0.89)
  Pallas kernels: 139 us -> 124 us
    pallas_call x1, Pallas kernels: 139 us -> 124 us  [body(): pl.pallas_call(kernel, out_shape=jax.ShapeDtypeStruct(nodes.shape, F32),...]
where the time goes in v4:
time: 128 us
  Pallas kernels  124 us (97%)
  local copies, waits for them, and re-layouts  4.05 us (3%)
    pallas_call x1, Pallas kernels, body(): pl.pallas_call(kernel, out_shape=jax.ShapeDtypeStruct(nodes.shape, F32),...  124 us
    unnamed x5, local copies, waits for them, and re-layouts  4.05 us

profile of v4, /device:TPU:120, one launch (start us, length us, event | category | flops | bytes accessed | tf_op | source)
XLA Modules:
  0.0 127.9 jit_solution(14902965761180726341)
XLA Ops:
  0.0 0.0 copy-start
  0.0 1.5 %copy-done = bf16[7,4,128,256]{3,2,1,0:T(8,128)(2,1)S(1)} copy-done((bf16[7,4,128,256]{3,2,1,0:T(8,128)(2,1)S(1)}, bf16[7,4,128,256]{3,2,1,0:T(8,128)(2,1)}, u32[]{:S(2)}) %copy-start) | copy-done | bytes 1835032
  1.5 0.0 copy-start.1
  1.5 1.4 %copy-done.1 = f32[1,3,4,128,256]{4,3,2,1,0:T(8,128)S(1)} copy-done((f32[1,3,4,128,256]{4,3,2,1,0:T(8,128)S(1)}, f32[1,3,4,128,256]{4,3,2,1,0:T(8,128)}, u32[]{:S(2)}) %copy-start.1) | copy-done | bytes 1572888
  2.9 123.8 %pfasst.1 = f32[1,3,4,128,256]{4,3,2,1,0:T(8,128)S(1)} custom-call(f32[1,3,4,128,256]{4,3,2,1,0:T(8,128)S(1)} %copy-done.1, bf16[7,4,128,256]{3,2,1,0:T(8,128)(2,1)S(1)} %copy-done), custom_call_target="tpu_custom_call" | custom-call | tf_op jit(solution)/shard_map/pfasst/pallas_call | solution.py:614
  126.7 1.1 copy.4
Async XLA Ops:
  0.0 1.5 %copy-start = (bf16[7,4,128,256]{3,2,1,0:T(8,128)(2,1)S(1)}, bf16[7,4,128,256]{3,2,1,0:T(8,128)(2,1)}, u32[]{:S(2)}) copy-start(bf16[7,4,128,256]{3,2,1,0:T(8,128)(2,1)} %coeffs_hbm.1) | copy-start | bytes 5505028
  1.5 1.4 %copy-start.1 = (f32[1,3,4,128,256]{4,3,2,1,0:T(8,128)S(1)}, f32[1,3,4,128,256]{4,3,2,1,0:T(8,128)}, u32[]{:S(2)}) copy-start(f32[1,3,4,128,256]{4,3,2,1,0:T(8,128)} %nodes_hbm.1) | copy-start | bytes 4718596

commit v5 on v4

--- a/solution.py
+++ b/solution.py
@@ -22,6 +22,11 @@
 NT = 32
 RIM = 8
 STRIP = 32
+FIRST = (0, 32, 64, 96, 128)
+SECOND = (0, 24, 56, 88, 128)
+THIRD = (0, 16, 48, 80, 128)
+FOURTH = (0, 0, 32, 64, 128)
+PIECES = 4
 WIN = 24
 DEEP = 24
 
@@ -169,30 +174,30 @@
     expect = expect + jnp.where(is_worker, last_block, 0) + jnp.where(is_worker & (block < last_block), hands, 0)
     pl.semaphore_wait(barrier, expect)
 
-    inner = pl.ds(RIM, ROWS)
-
-    def halo(buf, phase, upward):
+    def halo(buf, phase, bounds, i, upward):
+        rows = pl.ds(RIM + bounds[i], bounds[i + 1] - bounds[i])
         return pltpu.make_async_remote_copy(
-            src_ref=buf.at[DEPTH if upward else 1, inner],
-            dst_ref=buf.at[0 if upward else DEPTH + 1, inner],
-            send_sem=halo_s.at[phase, int(upward)],
-            recv_sem=halo_r.at[phase, int(upward)],
+            src_ref=buf.at[DEPTH if upward else 1, rows],
+            dst_ref=buf.at[0 if upward else DEPTH + 1, rows],
+            send_sem=halo_s.at[phase, int(upward), i],
+            recv_sem=halo_r.at[phase, int(upward), i],
             device_id=(t, s + 1 if upward else s - 1),
             device_id_type=MESH,
         )
 
-    def send_halo(buf, phase, upward):
+    def send_halo(buf, phase, bounds, i, upward):
         @pl.when(s < SLABS - 1 if upward else s > 0)
         def _():
-            halo(buf, phase, upward).start()
-
-    def take_halo(buf, phase, upward):
+            halo(buf, phase, bounds, i, upward).start()
+
+    def take_halo(buf, phase, bounds, i, upward):
         @pl.when(s > 0 if upward else s < SLABS - 1)
         def _():
-            halo(buf, phase, upward).wait_recv()
-
-    send_halo(ab, 0, False)
-    send_halo(ab, 0, True)
+            halo(buf, phase, bounds, i, upward).wait_recv()
+
+    for i in range(PIECES):
+        send_halo(ab, 0, FIRST, i, False)
+        send_halo(ab, 0, FIRST, i, True)
     for n in range(1, BLOCK):
         tell(known, base + lax.rem(place + n, BLOCK), s)
 
@@ -243,42 +248,36 @@
     loop(strips, lambda i: combine_a(1, i))
     loop(strips, lambda i: combine_a(2, i))
 
-    def force(buf, p, i):
-        window = pl.ds(pl.multiple_of(i * STRIP, STRIP), STRIP + 2 * RIM)
-        here = pl.ds(pl.multiple_of(i * STRIP, STRIP), STRIP)
+    def force(buf, p, low, rows):
+        window = slice(low, low + rows + 2 * RIM)
+        here = slice(low, low + rows)
         return stencil(
             buf[p, window, :], buf[p + 1, window, :], buf[p + 2, window, :],
-            [kf[m, p, here, :] for m in range(7)], STRIP + 2 * RIM, COLS, RIM, STRIP,
-        )
-
-    def spots(i):
-        return (
-            pl.ds(pl.multiple_of(i * STRIP, STRIP), STRIP),
-            pl.ds(pl.multiple_of(RIM + i * STRIP, 8), STRIP),
-        )
-
-    def first_node(p, i):
-        here, there = spots(i)
-        value = nodes[0, 0, p, here, :] + force(ab, p, i)
+            [kf[m, p, here, :] for m in range(7)], rows + 2 * RIM, COLS, RIM, rows,
+        )
+
+    def first_node(p, low, rows):
+        here = slice(low, low + rows)
+        value = nodes[0, 0, p, here, :] + force(ab, p, low, rows)
         v1[p, here, :] = value
-        bb[p + 1, there, :] = (
+        bb[p + 1, RIM + low : RIM + low + rows, :] = (
             0.1 * value + B0 * nodes[0, 0, p, here, :] + (B1 - 0.1) * nodes[0, 1, p, here, :] + B2 * nodes[0, 2, p, here, :]
         )
 
-    def last_node(p, i):
-        here, there = spots(i)
+    def last_node(p, low, rows):
+        here = slice(low, low + rows)
         first = v1[p, here, :]
-        value = first + force(bb, p, i)
+        value = first + force(bb, p, low, rows)
         v2[p, here, :] = value
-        cb[p + 1, there, :] = C0 * (nodes[0, 0, p, here, :] + value) + C1 * first
-
-    def add_force(p, i):
-        here, there = spots(i)
-        out[0, 0, p, here, :] = nodes[0, 0, p, here, :] + force(cb, p, i)
-
-    def planes(fn, which):
-        for p in which:
-            loop(strips, lambda i, p=p: fn(p, i))
+        cb[p + 1, RIM + low : RIM + low + rows, :] = C0 * (nodes[0, 0, p, here, :] + value) + C1 * first
+
+    def add_force(p, low, rows):
+        here = slice(low, low + rows)
+        out[0, 0, p, here, :] = nodes[0, 0, p, here, :] + force(cb, p, low, rows)
+
+    def piece(fn, p, bounds, i):
+        if bounds[i + 1] > bounds[i]:
+            fn(p, bounds[i], bounds[i + 1] - bounds[i])
 
     inside = slice(RIM, RIM + HALF)
     k = []
@@ -290,7 +289,9 @@
         kcp[m, inside, :] = 0.05 * k[m]
     kcp[5, inside, :] = 0.025 * k[5]
     kcp[6, inside, :] = 1.0 - (0.4 * k[0] + 0.1 * (k[1] + k[2]) + 0.2 * k[6])
-    planes(first_node, (1, 2))
+    for p in (1, 2):
+        for i in range(PIECES):
+            piece(first_node, p, FIRST, i)
     pl.semaphore_wait(known, BLOCK - 1)
 
     window = pl.ds(pl.multiple_of(8 * place, 8), WIN)
@@ -332,19 +333,24 @@
             device_id=(lax.rem(t + BLOCK * n, NT), s), device_id_type=MESH,
         )
 
-    take_halo(ab, 0, True)
-    planes(first_node, (0,))
-    send_halo(bb, 1, False)
-    take_halo(ab, 0, False)
-    planes(first_node, (3,))
-    send_halo(bb, 1, True)
-    planes(last_node, (1, 2))
-    take_halo(bb, 1, True)
-    planes(last_node, (0,))
-    send_halo(cb, 2, False)
-    take_halo(bb, 1, False)
-    planes(last_node, (3,))
-    send_halo(cb, 2, True)
+    for i in range(PIECES):
+        take_halo(ab, 0, FIRST, i, True)
+        piece(first_node, 0, SECOND, i)
+        send_halo(bb, 1, SECOND, i, False)
+        take_halo(ab, 0, FIRST, i, False)
+        piece(first_node, 3, SECOND, i)
+        send_halo(bb, 1, SECOND, i, True)
+        piece(last_node, 1, THIRD, i)
+        piece(last_node, 2, THIRD, i)
+    for i in range(PIECES):
+        take_halo(bb, 1, SECOND, i, True)
+        piece(last_node, 0, THIRD, i)
+        send_halo(cb, 2, THIRD, i, False)
+        take_halo(bb, 1, SECOND, i, False)
+        piece(last_node, 3, THIRD, i)
+        send_halo(cb, 2, THIRD, i, True)
+        piece(add_force, 1, FOURTH, i)
+        piece(add_force, 2, FOURTH, i)
 
     @pl.when(is_worker)
     def _():
@@ -359,18 +365,16 @@
     def _():
         send_v2.start()
 
-    planes(add_force, (1, 2))
-    take_halo(cb, 2, True)
-    planes(add_force, (0,))
-    take_halo(cb, 2, False)
-    planes(add_force, (3,))
-
     @pl.when(t < NT - 1)
     def _():
         send_w0.wait_recv()
 
-    for p in range(DEPTH):
-        rp[p, RIM : RIM + HALF, :] = average(p, out[0, 0, p]) - wn[p]
+    def right_side(p, low, rows):
+        half_rows = rows // 2
+        pairs[p, 0:rows] = times(out[0, 0, p, low : low + rows, :], narrow[...])
+        both = pairs[p, pl.ds(0, half_rows, stride=2), :] + pairs[p, pl.ds(1, half_rows, stride=2), :]
+        here = slice(low // 2, low // 2 + half_rows)
+        rp[p, RIM + low // 2 : RIM + low // 2 + half_rows, :] = both - wn[p, here, :]
 
     def send_r(z, j):
         to, at = worker(z, j)
@@ -384,8 +388,19 @@
         )
         return needed & own, needed & jnp.logical_not(own), copy, pltpu.make_async_copy(src, dst, r_r.at[place, s])
 
-    for z in (0, 1):
-        loop(SLABS, lambda j, z=z: start(send_r(z, j)))
+    done = 0
+    for i in range(PIECES):
+        take_halo(cb, 2, THIRD, i, True)
+        piece(add_force, 0, FOURTH, i)
+        take_halo(cb, 2, THIRD, i, False)
+        piece(add_force, 3, FOURTH, i)
+        for p in range(DEPTH):
+            piece(right_side, p, FOURTH, i)
+        ready = SLABS if i == PIECES - 1 else max(FOURTH[i + 1] // 16 - 1, 0)
+        if ready > done:
+            for z in (0, 1):
+                loop(ready - done, lambda j, z=z, done=done: start(send_r(z, done + j)))
+        done = ready
 
     @pl.when(jnp.logical_not(on_chip))
     def _():
@@ -495,13 +510,13 @@
             loop(count, arrived)
             low, low_y, low_x = slopes(hb[h, start_plane])[:3]
 
-            def group(i, carry):
+            def group(i, carry, planes):
                 (low, low_y, low_x), here = carry
-                for n in range(DEPTH):
+                for n in range(planes):
                     p = start_plane + DEPTH * i + n
                     above = slopes(hb[h, p + 2])
                     v, v_y, v_x, around_y, around_x, v_xy = here
-                    k = [kb[m, quad + i, n] for m in range(7)]
+                    k = [kb[m, quad + i + n // DEPTH, n % DEPTH] for m in range(7)]
                     total = rb[h, p] + k[0] * (above[0] + low) + k[1] * around_x + k[2] * around_y
                     total = total + k[3] * (above[2] - low_x) + k[4] * (above[1] - low_y)
                     hb[h + 1, p + 1] = total + k[5] * v_xy + k[6] * v
@@ -509,7 +524,11 @@
                     here = above
                 return (low, low_y, low_x), here
 
-            lax.fori_loop(0, count, group, ((low, low_y, low_x), slopes(hb[h, start_plane + 1])))
+            for some in (6, 5, 4):
+
+                @pl.when(count == some)
+                def _(some=some):
+                    group(0, ((low, low_y, low_x), slopes(hb[h, start_plane + 1])), DEPTH * some)
 
             @pl.when(block == last_block)
             def _():
@@ -554,15 +573,16 @@
             out[0, 0, p] += gain
             out[0, 1, p] += 0.5 * gain
 
-    for phase, buf in enumerate((ab, bb, cb)):
-
-        @pl.when(s < SLABS - 1)
-        def _(phase=phase, buf=buf):
-            halo(buf, phase, True).wait_send()
-
-        @pl.when(s > 0)
-        def _(phase=phase, buf=buf):
-            halo(buf, phase, False).wait_send()
+    for phase, (buf, bounds) in enumerate(((ab, FIRST), (bb, SECOND), (cb, THIRD))):
+        for i in range(PIECES):
+
+            @pl.when(s < SLABS - 1)
+            def _(phase=phase, buf=buf, bounds=bounds, i=i):
+                halo(buf, phase, bounds, i, True).wait_send()
+
+            @pl.when(s > 0)
+            def _(phase=phase, buf=buf, bounds=bounds, i=i):
+                halo(buf, phase, bounds, i, False).wait_send()
 
     @pl.when(t > 0)
     def _():
@@ -610,7 +630,7 @@
         (7, DEEP // DEPTH, DEPTH, WIN, LANES), (BLOCK, DEEP, WIN, LANES), (BLOCK + 1, DEEP + 2, WIN, LANES), coarse, coarse,
         (DEPTH, ROWS, LANES),
     ]
-    sems = [(3, 2), (3, 2), (2,), (2,), (2,), (1,), (2, 8), (8, 8), (2, 3), (2, 3), (8, 4), (1,), (1,), (1,), (2,), (3,), (4,)]
+    sems = [(3, 2, PIECES), (3, 2, PIECES), (2,), (2,), (2,), (1,), (2, 8), (8, 8), (2, 3), (2, 3), (8, 4), (1,), (1,), (1,), (2,), (3,), (4,)]
     return pl.pallas_call(
         kernel,
         out_shape=jax.ShapeDtypeStruct(nodes.shape, F32),

time: 128 us -> 115 us (0.90)
  Pallas kernels: 124 us -> 110 us
    pallas_call x1, Pallas kernels: 124 us -> 110 us  [body(): pl.pallas_call(kernel, out_shape=jax.ShapeDtypeStruct(nodes.shape, F32),...]
where the time goes in v5:
time: 115 us; the launch traced here: 114 us
  Pallas kernels  110 us (96%)
  local copies, waits for them, and re-layouts  4.05 us (4%)
    pallas_call x1, Pallas kernels, body(): pl.pallas_call(kernel, out_shape=jax.ShapeDtypeStruct(nodes.shape, F32),...  110 us
    unnamed x5, local copies, waits for them, and re-layouts  4.05 us

profile of v5, /device:TPU:120, one launch (start us, length us, event | category | flops | bytes accessed | tf_op | source)
XLA Modules:
  0.0 114.1 jit_solution(14499892874590349469)
XLA Ops:
  0.0 0.0 copy-start
  0.0 1.5 %copy-done = bf16[7,4,128,256]{3,2,1,0:T(8,128)(2,1)S(1)} copy-done((bf16[7,4,128,256]{3,2,1,0:T(8,128)(2,1)S(1)}, bf16[7,4,128,256]{3,2,1,0:T(8,128)(2,1)}, u32[]{:S(2)}) %copy-start) | copy-done | bytes 1835032
  1.5 0.0 copy-start.1
  1.5 1.4 %copy-done.1 = f32[1,3,4,128,256]{4,3,2,1,0:T(8,128)S(1)} copy-done((f32[1,3,4,128,256]{4,3,2,1,0:T(8,128)S(1)}, f32[1,3,4,128,256]{4,3,2,1,0:T(8,128)}, u32[]{:S(2)}) %copy-start.1) | copy-done | bytes 1572888
  2.9 110.0 %pfasst.1 = f32[1,3,4,128,256]{4,3,2,1,0:T(8,128)S(1)} custom-call(f32[1,3,4,128,256]{4,3,2,1,0:T(8,128)S(1)} %copy-done.1, bf16[7,4,128,256]{3,2,1,0:T(8,128)(2,1)S(1)} %copy-done), custom_call_target="tpu_custom_call" | custom-call | tf_op jit(solution)/shard_map/pfasst/pallas_call | solution.py:634
  112.9 1.1 %copy.4 = f32[1,3,4,128,256]{4,3,2,1,0:T(8,128)} copy(f32[1,3,4,128,256]{4,3,2,1,0:T(8,128)S(1)} %pfasst.1) | data formatting | bytes 3145728
Async XLA Ops:
  0.0 1.5 %copy-start = (bf16[7,4,128,256]{3,2,1,0:T(8,128)(2,1)S(1)}, bf16[7,4,128,256]{3,2,1,0:T(8,128)(2,1)}, u32[]{:S(2)}) copy-start(bf16[7,4,128,256]{3,2,1,0:T(8,128)(2,1)} %coeffs_hbm.1) | copy-start | bytes 5505028
  1.5 1.4 %copy-start.1 = (f32[1,3,4,128,256]{4,3,2,1,0:T(8,128)S(1)}, f32[1,3,4,128,256]{4,3,2,1,0:T(8,128)}, u32[]{:S(2)}) copy-start(f32[1,3,4,128,256]{4,3,2,1,0:T(8,128)} %nodes_hbm.1) | copy-start | bytes 4718596

commit v6 on v5

--- a/solution.py
+++ b/solution.py
@@ -32,8 +32,7 @@
 
 
 def worker(half, j):
-    odd = lax.rem(j, 2)
-    return 2 * lax.rem(j, 4), 2 * jnp.where(half == 0, odd, 3 - odd) + lax.div(j, 4)
+    return 2 * lax.rem(j, 4), 2 * (1 + half) + lax.div(j, 4)
 
 
 def neighbours(value, axis, size, mask_low, mask_high):
@@ -96,8 +95,7 @@
     base = block * BLOCK
     half = lax.div(s, 4)
     chunk = 4 * lax.rem(s, 2) + lax.div(place, 2)
-    odd = lax.rem(lax.div(s, 2), 2)
-    is_worker = (lax.rem(place, 2) == 0) & (lax.rem(chunk, 2) == jnp.where(half == 0, odd, 1 - odd))
+    is_worker = (lax.rem(place, 2) == 0) & (lax.div(s, 2) == 1 + half)
     last_block = NT // BLOCK - 1
     strips = ROWS // STRIP
 
@@ -357,7 +355,10 @@
         part = kb.at[:, :, block]
         pltpu.make_async_copy(part, part, k_r.at[0]).wait()
         for n in range(1, NT // BLOCK):
-            pass_k(n).start()
+
+            @pl.when(block == NT // BLOCK - n)
+            def _(n=n):
+                pass_k(n).start()
 
     on_chip = lax.rem(place, 2) == 0
 
@@ -402,6 +403,14 @@
                 loop(ready - done, lambda j, z=z, done=done: start(send_r(z, done + j)))
         done = ready
 
+    @pl.when(is_worker)
+    def _():
+        for n in range(1, NT // BLOCK):
+
+            @pl.when(block != NT // BLOCK - n)
+            def _(n=n):
+                pass_k(n).start()
+
     @pl.when(jnp.logical_not(on_chip))
     def _():
         for z in (0, 1):
@@ -511,15 +520,17 @@
             low, low_y, low_x = slopes(hb[h, start_plane])[:3]
 
             def group(i, carry, planes):
+                rows = slice(8, 16) if planes == 4 * DEPTH else slice(0, WIN)
                 (low, low_y, low_x), here = carry
                 for n in range(planes):
                     p = start_plane + DEPTH * i + n
                     above = slopes(hb[h, p + 2])
                     v, v_y, v_x, around_y, around_x, v_xy = here
-                    k = [kb[m, quad + i + n // DEPTH, n % DEPTH] for m in range(7)]
-                    total = rb[h, p] + k[0] * (above[0] + low) + k[1] * around_x + k[2] * around_y
-                    total = total + k[3] * (above[2] - low_x) + k[4] * (above[1] - low_y)
-                    hb[h + 1, p + 1] = total + k[5] * v_xy + k[6] * v
+                    k = [kb[m, quad + i + n // DEPTH, n % DEPTH, rows, :] for m in range(7)]
+                    cut = lambda a: a[rows]
+                    total = rb[h, p, rows, :] + k[0] * cut(above[0] + low) + k[1] * cut(around_x) + k[2] * cut(around_y)
+                    total = total + k[3] * cut(above[2] - low_x) + k[4] * cut(above[1] - low_y)
+                    hb[h + 1, p + 1, rows, :] = total + k[5] * cut(v_xy) + k[6] * cut(v)
                     low, low_y, low_x = v, v_y, v_x
                     here = above
                 return (low, low_y, low_x), here
@@ -538,13 +549,12 @@
 
         @pl.when(block < last_block)
         def _():
-            for dj in (-1, 0, 1):
+            for z, dj in ((1, -1), (1, 1), (0, -1), (0, 1), (1, 0), (0, 0)):
                 j = chunk + dj
 
                 @pl.when((j >= 0) & (j < SLABS))
-                def _(dj=dj):
-                    hand(0, dj).start()
-                    hand(1, dj).start()
+                def _(z=z, dj=dj):
+                    hand(z, dj).start()
 
             loop(BLOCK, start_spread)
 

time: 115 us -> 113 us (0.983)
  Pallas kernels: 110 us -> 108 us
    pallas_call x1, Pallas kernels: 110 us -> 108 us  [body(): pl.pallas_call(kernel, out_shape=jax.ShapeDtypeStruct(nodes.shape, F32),...]
where the time goes in v6:
time: 113 us
  Pallas kernels  108 us (96%)
  local copies, waits for them, and re-layouts  4.05 us (4%)
    pallas_call x1, Pallas kernels, body(): pl.pallas_call(kernel, out_shape=jax.ShapeDtypeStruct(nodes.shape, F32),...  108 us
    unnamed x5, local copies, waits for them, and re-layouts  4.05 us

profile of v6, /device:TPU:120, one launch (start us, length us, event | category | flops | bytes accessed | tf_op | source)
XLA Modules:
  0.0 112.5 jit_solution(11438700176960715708)
XLA Ops:
  0.0 0.0 copy-start
  0.0 1.5 %copy-done = bf16[7,4,128,256]{3,2,1,0:T(8,128)(2,1)S(1)} copy-done((bf16[7,4,128,256]{3,2,1,0:T(8,128)(2,1)S(1)}, bf16[7,4,128,256]{3,2,1,0:T(8,128)(2,1)}, u32[]{:S(2)}) %copy-start) | copy-done | bytes 1835032
  1.5 0.0 copy-start.1
  1.5 1.4 %copy-done.1 = f32[1,3,4,128,256]{4,3,2,1,0:T(8,128)S(1)} copy-done((f32[1,3,4,128,256]{4,3,2,1,0:T(8,128)S(1)}, f32[1,3,4,128,256]{4,3,2,1,0:T(8,128)}, u32[]{:S(2)}) %copy-start.1) | copy-done | bytes 1572888
  2.9 108.5 %pfasst.1 = f32[1,3,4,128,256]{4,3,2,1,0:T(8,128)S(1)} custom-call(f32[1,3,4,128,256]{4,3,2,1,0:T(8,128)S(1)} %copy-done.1, bf16[7,4,128,256]{3,2,1,0:T(8,128)(2,1)S(1)} %copy-done), custom_call_target="tpu_custom_call" | custom-call | tf_op jit(solution)/shard_map/pfasst/pallas_call | solution.py:644
  111.4 1.1 %copy.4 = f32[1,3,4,128,256]{4,3,2,1,0:T(8,128)} copy(f32[1,3,4,128,256]{4,3,2,1,0:T(8,128)S(1)} %pfasst.1) | data formatting | bytes 3145728
Async XLA Ops:
  0.0 1.5 %copy-start = (bf16[7,4,128,256]{3,2,1,0:T(8,128)(2,1)S(1)}, bf16[7,4,128,256]{3,2,1,0:T(8,128)(2,1)}, u32[]{:S(2)}) copy-start(bf16[7,4,128,256]{3,2,1,0:T(8,128)(2,1)} %coeffs_hbm.1) | copy-start | bytes 5505028
  1.5 1.4 %copy-start.1 = (f32[1,3,4,128,256]{4,3,2,1,0:T(8,128)S(1)}, f32[1,3,4,128,256]{4,3,2,1,0:T(8,128)}, u32[]{:S(2)}) copy-start(f32[1,3,4,128,256]{4,3,2,1,0:T(8,128)} %nodes_hbm.1) | copy-start | bytes 4718596

commit v7 on v6

--- a/solution.py
+++ b/solution.py
@@ -379,7 +379,7 @@
 
     def send_r(z, j):
         to, at = worker(z, j)
-        src = rp.at[:, pl.ds(pl.multiple_of(8 * j, 8), WIN)]
+        src = rp.at[:, pl.ds(8 * j if isinstance(j, int) else pl.multiple_of(8 * j, 8), WIN)]
         dst = rb.at[place, pl.ds(DEPTH * s - 8 * z, DEPTH)]
         own = (to == place) & (at == s)
         needed = DEPTH * s + 3 >= 9 + place if z else DEPTH * s < 23 - place
@@ -400,7 +400,8 @@
         ready = SLABS if i == PIECES - 1 else max(FOURTH[i + 1] // 16 - 1, 0)
         if ready > done:
             for z in (0, 1):
-                loop(ready - done, lambda j, z=z, done=done: start(send_r(z, done + j)))
+                for j in range(done, ready):
+                    start(send_r(z, j))
         done = ready
 
     @pl.when(is_worker)
@@ -464,7 +465,8 @@
         return own, jnp.logical_not(own), copy, pltpu.make_async_copy(src, dst, e_r.at[0])
 
     def start_spread(h):
-        loop(4, lambda n: start(spread(h, n)))
+        for n in range(SLABS // 2):
+            start(spread(h, n))
 
     @pl.when(is_worker)
     def _():
@@ -473,10 +475,6 @@
             hb[h, DEEP + 1] = jnp.zeros((WIN, LANES), F32)
 
         loop(BLOCK + 1, clear)
-
-        @pl.when(block == 0)
-        def _():
-            hb[0, 1 : DEEP + 1] = jnp.zeros((DEEP, WIN, LANES), F32)
 
         @pl.when((block > 0) & (chunk == 0))
         def _():
@@ -517,7 +515,10 @@
                 pltpu.make_async_copy(part, part, r_r.at[h, slab0 + i]).wait()
 
             loop(count, arrived)
-            low, low_y, low_x = slopes(hb[h, start_plane])[:3]
+
+            def below():
+                return slopes(hb[h, start_plane])[:3]
+
 
             def group(i, carry, planes):
                 rows = slice(8, 16) if planes == 4 * DEPTH else slice(0, WIN)
@@ -535,11 +536,17 @@
                     here = above
                 return (low, low_y, low_x), here
 
+            since = jnp.where(block == 0, 1, 0)
+
+            @pl.when(h < since)
+            def _():
+                hb[1, 1 : DEEP + 1] = rb[0]
+
             for some in (6, 5, 4):
 
-                @pl.when(count == some)
+                @pl.when((count == some) & (h >= since))
                 def _(some=some):
-                    group(0, ((low, low_y, low_x), slopes(hb[h, start_plane + 1])), DEPTH * some)
+                    group(0, (below(), slopes(hb[h, start_plane + 1])), DEPTH * some)
 
             @pl.when(block == last_block)
             def _():

time: 113 us -> 112 us (level)
  no operation moved by 1% of the time
where the time goes in v7:
time: 112 us
  Pallas kernels  108 us (96%)
  local copies, waits for them, and re-layouts  4.05 us (4%)
    pallas_call x1, Pallas kernels, body(): pl.pallas_call(kernel, out_shape=jax.ShapeDtypeStruct(nodes.shape, F32),...  108 us
    unnamed x5, local copies, waits for them, and re-layouts  4.05 us

profile of v7, /device:TPU:120, one launch (start us, length us, event | category | flops | bytes accessed | tf_op | source)
XLA Modules:
  0.0 111.7 jit_solution(17091714840896467824)
XLA Ops:
  0.0 0.0 copy-start
  0.0 1.5 %copy-done = bf16[7,4,128,256]{3,2,1,0:T(8,128)(2,1)S(1)} copy-done((bf16[7,4,128,256]{3,2,1,0:T(8,128)(2,1)S(1)}, bf16[7,4,128,256]{3,2,1,0:T(8,128)(2,1)}, u32[]{:S(2)}) %copy-start) | copy-done | bytes 1835032
  1.5 0.0 copy-start.1
  1.5 1.4 %copy-done.1 = f32[1,3,4,128,256]{4,3,2,1,0:T(8,128)S(1)} copy-done((f32[1,3,4,128,256]{4,3,2,1,0:T(8,128)S(1)}, f32[1,3,4,128,256]{4,3,2,1,0:T(8,128)}, u32[]{:S(2)}) %copy-start.1) | copy-done | bytes 1572888
  2.9 107.7 %pfasst.1 = f32[1,3,4,128,256]{4,3,2,1,0:T(8,128)S(1)} custom-call(f32[1,3,4,128,256]{4,3,2,1,0:T(8,128)S(1)} %copy-done.1, bf16[7,4,128,256]{3,2,1,0:T(8,128)(2,1)S(1)} %copy-done), custom_call_target="tpu_custom_call" | custom-call | tf_op jit(solution)/shard_map/pfasst/pallas_call | solution.py:651
  110.6 1.1 %copy.4 = f32[1,3,4,128,256]{4,3,2,1,0:T(8,128)} copy(f32[1,3,4,128,256]{4,3,2,1,0:T(8,128)S(1)} %pfasst.1) | data formatting | bytes 3145728
Async XLA Ops:
  0.0 1.5 %copy-start = (bf16[7,4,128,256]{3,2,1,0:T(8,128)(2,1)S(1)}, bf16[7,4,128,256]{3,2,1,0:T(8,128)(2,1)}, u32[]{:S(2)}) copy-start(bf16[7,4,128,256]{3,2,1,0:T(8,128)(2,1)} %coeffs_hbm.1) | copy-start | bytes 5505028
  1.5 1.4 %copy-start.1 = (f32[1,3,4,128,256]{4,3,2,1,0:T(8,128)S(1)}, f32[1,3,4,128,256]{4,3,2,1,0:T(8,128)}, u32[]{:S(2)}) copy-start(f32[1,3,4,128,256]{4,3,2,1,0:T(8,128)} %nodes_hbm.1) | copy-start | bytes 4718596
